TPU v7x, 512 devices: a whole 4x4x16 slice. The times are simulated.
512 devices in a mesh: col: 512 (over x, z, y, core).
Axes of the slice: x: 4, y: 4, z: 16, core: 2. Of those that a mesh axis runs over, the one named last changes fastest.
Arguments:
- final_adjoint: float32 [7, 50, 65536], P(None, None, 'col'), may hold values from -6 to 6
- states: float32 [3, 7, 50, 65536], P(None, None, None, 'col'), may hold values from 0.05 to 3
- implicit: float32 [50, 50, 65536], P(None, None, 'col'), may hold values from -0.6 to 1
- wet_levels: int32 [65536], P('col'), may hold values from 12 to 50
- tile_rows: int32 [15360], P('col'), may hold values from 0 to 25599, as said below
- tile_cols: int32 [15360], P('col'), may hold values from 0 to 25599, as said below
- tiles: bfloat16 [15360, 128, 128], P('col'), may hold values from -0.3984375 to 0.3984375
- tile_count: int32 [512], P('col'), may hold values from 5 to 30, as said below
Outputs:
- initial_adjoint: float32 [7, 50, 65536], P(None, None, 'col')
Inputs may be any that keep to these rules, and one draw needn't show every extreme that they name: `tile_rows`: a tile slot of device d names a row block of device d. `tile_cols`: a tile's column block lies on a device at most 2 away from the device of its row block. Slots from tile_count on are not part of the matrix; some device fills all 30 slots.
All inputs are finite; a program needn't handle non-finite values.
Results may differ from a plain program's by a relative error of at most 0.0003.
Values sent between devices are 32-bit elements; how exact they have to be, the bound alone decides.
No kernel may reach another device: no remote copies, remote signals or barrier semaphores. Data moves between devices by JAX's collectives and lax.ppermute only.
A program may use at most 64 MiB of HBM per device.

v0:
```python
import jax
import jax.numpy as jnp
from jax import lax
from jax.sharding import PartitionSpec as P

STEPS = 3
REACH = 2


time_step = 0.5


def shifted(value, axis, by):
    peers = lax.axis_size(axis)
    pairs = [(i, i + by) for i in range(peers) if 0 <= i + by < peers]
    return lax.ppermute(value, axis, pairs)


def sources(state, light_factor):
    phosphate, dissolved, oxygen, plankton, grazers, detritus, nitrate = [
        state[i] for i in range(7)
    ]
    growth = (
        1.2 * light_factor * plankton * phosphate / (0.03 + phosphate) * nitrate / (0.5 + nitrate)
    )
    grazing = 1.9 * grazers * plankton * plankton / (0.1 + plankton * plankton)
    mortality = 0.03 * plankton * plankton
    remineral = 0.05 * detritus * oxygen / (1.0 + oxygen)
    dop_decay = 0.17 * dissolved
    grazer_loss = 0.05 * grazers * grazers
    return jnp.stack(
        [
            -growth + remineral + dop_decay + 0.3 * grazing,
            0.1 * growth + 0.1 * mortality - dop_decay,
            1.2 * (growth - remineral - dop_decay),
            growth - grazing - mortality,
            0.7 * grazing - grazer_loss,
            grazer_loss + 0.9 * mortality - remineral,
            1.6 * (remineral + dop_decay - growth),
        ]
    )


def shards(final_adjoint, states, implicit, wet_levels, tile_rows, tile_cols, tiles, tile_count):
    tracers, levels, width = final_adjoint.shape
    blocks_dev = levels * width // 128
    slot_count = tiles.shape[0]
    targets = (2 * REACH + 1) * blocks_dev
    highest = lax.Precision.HIGHEST
    device = lax.axis_index("col")
    level_ids = lax.broadcasted_iota(jnp.int32, (levels, width), 0)
    wet_mask = (level_ids < wet_levels[None, :]).astype(jnp.float32)
    light_factor = jnp.exp(
        -0.2 * lax.broadcasted_iota(jnp.int32, (levels, 1), 0).astype(jnp.float32)
    )
    row_local = tile_rows - device * blocks_dev
    col_slot = (tile_cols // blocks_dev - device + REACH) * blocks_dev + tile_cols % blocks_dev
    active = lax.broadcasted_iota(jnp.int32, (slot_count,), 0) < tile_count[0]
    block_marks = lax.broadcasted_iota(jnp.int32, (blocks_dev,), 0).astype(jnp.float32)
    wide_tiles = tiles.astype(jnp.float32)
    pick_rows = (
        row_local[:, None] == lax.broadcasted_iota(jnp.int32, (slot_count, blocks_dev), 1)
    ).astype(jnp.float32)
    place_cols = (
        (col_slot[:, None] == lax.broadcasted_iota(jnp.int32, (slot_count, targets), 1))
        & active[:, None]
    ).astype(jnp.float32)
    adjoint = final_adjoint
    for section in range(STEPS - 1, -1, -1):
        carried = jnp.einsum("klc,tkc->tlc", implicit, adjoint, precision=highest) * wet_mask
        picked = jnp.einsum("sb,tbi->tsi", pick_rows, carried, precision=highest)
        terms = jnp.einsum("tsi,sij->tsj", picked, wide_tiles, precision=highest)
        partial_value = jnp.einsum("sn,tsj->tnj", place_cols, terms, precision=highest)
        partial_value = partial_value.reshape(tracers, 2 * REACH + 1, blocks_dev, 128)
        own_sum = partial_value[:, 2]
        up_one = (partial_value[:, 3], block_marks)
        up_two = (partial_value[:, 4], block_marks)
        down_one = (partial_value[:, 1], block_marks)
        down_two = (partial_value[:, 0], block_marks)
        got_below = shifted((up_one[0], up_one[1]), "col", 1)
        got_above = shifted((down_one[0], down_one[1]), "col", -1)
        got_far_below = shifted((up_two[0], up_two[1]), "col", 2)
        got_far_above = shifted((down_two[0], down_two[1]), "col", -2)
        from_below = got_below[0]
        from_above = got_above[0]
        far_below = got_far_below[0]
        far_above = got_far_above[0]
        summed = own_sum + from_below + from_above + far_below + far_above
        unused, pull_back = jax.vjp(lambda state: sources(state, light_factor), states[section])
        biology = pull_back(carried)[0]
        adjoint = wet_mask * (carried + summed + time_step * biology)
    return adjoint


def solution(mesh):
    in_specs = (
        P(None, None, "col"),
        P(None, None, None, "col"),
        P(None, None, "col"),
        P("col"),
        P("col"),
        P("col"),
        P("col", None, None),
        P("col"),
    )
    out_specs = P(None, None, "col")
    return jax.shard_map(shards, mesh=mesh, in_specs=in_specs, out_specs=out_specs, check_vma=False)
```

profile of v0, /device:TPU:7, one launch (start us, length us, event | category | flops | bytes accessed | tf_op | source)
XLA Modules:
  0.0 112.3 jit_solution(7510297709667125574)
XLA Ops:
  0.8 0.7 fusion.73
  1.4 0.7 fusion.32
  2.1 1.2 %copy.171 = f32[7,50,128]{1,0,2:T(8,128)S(1)} copy(f32[7,50,128]{2,1,0:T(8,128)} %param.8) | data formatting | bytes 358400 | tf_op args[0]
  3.3 5.5 %copy.172 = f32[50,50,128]{1,0,2:T(8,128)} copy(f32[50,50,128]{2,1,0:T(8,128)} %param.10) | data formatting | bytes 2560000 | tf_op args[2]
  8.7 5.3 %fusion.75 = f32[128,7,50]{2,1,0:T(8,128)S(1)} fusion(f32[7,50,128]{1,0,2:T(8,128)S(1)} %copy.171, f32[50,50,128]{1,0,2:T(8,128)} %copy.172), kind=kOutput, calls=%fused_computation.197 | convolution fusion | flops 26880000 | bytes 1638400 | tf_op jit(solution)/shard_map/klc,tkc->tlc/dot_general | solution.py:70
  14.1 0.2 copy.173
  14.4 0.3 convolution_bitcast_fusion.8
  14.6 0.9 convolution_bitcast_fusion.5
  15.5 0.6 convolution_bitcast_fusion.2
  16.1 0.4 copy.226
  16.6 0.1 slice_bitcast_fusion.13
  16.6 3.8 %collective-permute-start = (f32[7,50,128]{2,0,1:T(8,128)S(1)}, f32[7,50,128]{2,0,1:T(8,128)S(1)}, u32[]{:S(2)}, u32[]{:S(2)}) collective-permute-start(f32[7,50,128]{2,0,1:T(8,128)S(1)} %get-tuple-element.34), channel_id=1, source_target_pairs={{0,1},{1,2},{2,3},{3,4},{4,5},{5,6},{6,7},{7,8},{8,9},{9,10},{10,1... | collective-permute-start | bytes 537608 | tf_op jit(solution)/shard_map/ppermute | solution.py:16
  20.4 12.0 %collective-permute-start.3 = (f32[7,50,128]{2,0,1:T(8,128)S(1)}, f32[7,50,128]{2,0,1:T(8,128)S(1)}, u32[]{:S(2)}, u32[]{:S(2)}) collective-permute-start(f32[7,50,128]{2,0,1:T(8,128)S(1)} %get-tuple-element.35), channel_id=1, source_target_pairs={{2,0},{3,1},{4,2},{5,3},{6,4},{7,5},{8,6},{9,7},{10,8},{11,9},{12,... | collective-permute-start | bytes 537608 | tf_op jit(solution)/shard_map/ppermute | solution.py:16
  32.4 1.9 %collective-permute-start.2 = (f32[7,50,128]{2,0,1:T(8,128)S(1)}, f32[7,50,128]{2,0,1:T(8,128)S(1)}, u32[]{:S(2)}, u32[]{:S(2)}) collective-permute-start(f32[7,50,128]{2,0,1:T(8,128)S(1)} %get-tuple-element.36), channel_id=1, source_target_pairs={{0,2},{1,3},{2,4},{3,5},{4,6},{5,7},{6,8},{7,9},{8,10},{9,11},{10,... | collective-permute-start | bytes 537608 | tf_op jit(solution)/shard_map/ppermute | solution.py:16
  34.3 3.0 %collective-permute-start.1 = (f32[7,50,128]{2,0,1:T(8,128)S(1)}, f32[7,50,128]{2,0,1:T(8,128)S(1)}, u32[]{:S(2)}, u32[]{:S(2)}) collective-permute-start(f32[7,50,128]{2,0,1:T(8,128)S(1)} %get-tuple-element.37), channel_id=1, source_target_pairs={{1,0},{2,1},{3,2},{4,3},{5,4},{6,5},{7,6},{8,7},{9,8},{10,9},{11,1... | collective-permute-start | bytes 537608 | tf_op jit(solution)/shard_map/ppermute | solution.py:16
  37.4 1.7 %fusion.74 = (f32[1,1,50,128]{3,2,1,0:T(8,128)}, f32[1,1,50,128]{3,2,1,0:T(8,128)}, f32[1,1,50,128]{3,2,1,0:T(8,128)S(1)}, f32[1,1,50,128]{3,2,1,0:T(8,128)S(1)}...) fusion(f32[3,7,50,128]{3,2,1,0:T(8,128)} %param.9), kind=kLoop, calls=%fused_computation.196 | loop fusion | flops 19200 | bytes 921600 | tf_op jit(solution)/shard_map/jvp()/slice | solution.py:21
  39.1 0.3 multiply_add_fusion.17
  39.4 0.2 multiply_add_fusion.20
  39.6 0.1 multiply_add_fusion.14
  39.7 0.4 multiply_multiply_fusion.2
  40.1 0.1 multiply_add_fusion.15
  40.2 0.0 collective-permute-done
  40.2 3.9 %collective-permute-done.2 = f32[7,50,128]{2,0,1:T(8,128)S(1)} collective-permute-done((f32[7,50,128]{2,0,1:T(8,128)S(1)}, f32[7,50,128]{2,0,1:T(8,128)S(1)}, u32[]{:S(2)}, u32[]{:S(2)}) %collective-permute-start.2) | collective-permute-done | bytes 179232 | tf_op jit(solution)/shard_map/ppermute | solution.py:16
  44.2 0.0 collective-permute-done.1
  44.2 0.3 fusion.20
  44.4 0.3 copy.189
  44.7 5.3 %fusion.76 = f32[128,7,50]{2,1,0:T(8,128)S(1)} fusion(f32[7,50,128]{1,0,2:T(8,128)S(1)} %copy.189, f32[50,50,128]{1,0,2:T(8,128)} %copy.172), kind=kOutput, calls=%fused_computation.198 | convolution fusion | flops 26880000 | bytes 1638400 | tf_op jit(solution)/shard_map/klc,tkc->tlc/dot_general | solution.py:70
  50.0 0.2 copy.191
  50.3 0.2 convolution_bitcast_fusion.7
  50.6 0.9 multiply_add_fusion.10
  51.5 0.8 multiply_add_fusion.13
  52.3 0.6 copy-done.4
  52.9 0.7 multiply_add_fusion.7
  53.6 0.9 convolution_bitcast_fusion.4
  54.5 0.6 convolution_bitcast_fusion.1
  55.1 0.4 copy.228
  55.5 0.1 slice_bitcast_fusion.8
  55.6 1.9 %collective-permute-start.4 = (f32[7,50,128]{2,0,1:T(8,128)S(1)}, f32[7,50,128]{2,0,1:T(8,128)S(1)}, u32[]{:S(2)}, u32[]{:S(2)}) collective-permute-start(f32[7,50,128]{2,0,1:T(8,128)S(1)} %get-tuple-element.30), channel_id=1, source_target_pairs={{0,1},{1,2},{2,3},{3,4},{4,5},{5,6},{6,7},{7,8},{8,9},{9,10},{10,1... | collective-permute-start | bytes 537608 | tf_op jit(solution)/shard_map/ppermute | solution.py:16
  57.5 9.3 %collective-permute-start.7 = (f32[7,50,128]{2,0,1:T(8,128)S(1)}, f32[7,50,128]{2,0,1:T(8,128)S(1)}, u32[]{:S(2)}, u32[]{:S(2)}) collective-permute-start(f32[7,50,128]{2,0,1:T(8,128)S(1)} %get-tuple-element.31), channel_id=1, source_target_pairs={{2,0},{3,1},{4,2},{5,3},{6,4},{7,5},{8,6},{9,7},{10,8},{11,9},{12,... | collective-permute-start | bytes 537608 | tf_op jit(solution)/shard_map/ppermute | solution.py:16
  66.9 1.9 %collective-permute-start.6 = (f32[7,50,128]{2,0,1:T(8,128)S(1)}, f32[7,50,128]{2,0,1:T(8,128)S(1)}, u32[]{:S(2)}, u32[]{:S(2)}) collective-permute-start(f32[7,50,128]{2,0,1:T(8,128)S(1)} %get-tuple-element.32), channel_id=1, source_target_pairs={{0,2},{1,3},{2,4},{3,5},{4,6},{5,7},{6,8},{7,9},{8,10},{9,11},{10,... | collective-permute-start | bytes 537608 | tf_op jit(solution)/shard_map/ppermute | solution.py:16
  68.8 2.6 %collective-permute-start.5 = (f32[7,50,128]{2,0,1:T(8,128)S(1)}, f32[7,50,128]{2,0,1:T(8,128)S(1)}, u32[]{:S(2)}, u32[]{:S(2)}) collective-permute-start(f32[7,50,128]{2,0,1:T(8,128)S(1)} %get-tuple-element.33), channel_id=1, source_target_pairs={{1,0},{2,1},{3,2},{4,3},{5,4},{6,5},{7,6},{8,7},{9,8},{10,9},{11,1... | collective-permute-start | bytes 537608 | tf_op jit(solution)/shard_map/ppermute | solution.py:16
  71.4 1.2 %multiply_multiply_fusion.1 = (f32[1,50,128]{2,0,1:T(1,128)S(1)}, f32[1,50,128]{2,0,1:T(1,128)S(1)}, f32[1,50,128]{2,0,1:T(1,128)S(1)}, f32[1,50,128]{2,0,1:T(1,128)S(1)}) fusion(f32[1,1,50,128]{3,2,1,0:T(8,128)} %get-tuple-element.45, f32[7,50,128]{2,0,1:T(8,128)S(1)} %bitcast_multiply_fusion.1, f32[1,1,50,128]{3,2,1,0:T(8,128)S(1)} %get-tuple-element.46, ...), kind=kLoop, calls=%fused_computation.140 | loop fusion | flops 294400 | bytes 435400 | tf_op jit(solution)/shard_map/transpose(jvp())/mul | solution.py:28
  72.6 0.8 multiply_add_fusion.8
  73.5 5.6 %collective-permute-done.6 = f32[7,50,128]{2,0,1:T(8,128)S(1)} collective-permute-done((f32[7,50,128]{2,0,1:T(8,128)S(1)}, f32[7,50,128]{2,0,1:T(8,128)S(1)}, u32[]{:S(2)}, u32[]{:S(2)}) %collective-permute-start.6) | collective-permute-done | bytes 179232 | tf_op jit(solution)/shard_map/ppermute | solution.py:16
  79.1 1.0 fusion.13
  80.2 0.3 copy.207
  80.4 5.3 %fusion.77 = f32[128,7,50]{2,1,0:T(8,128)S(1)} fusion(f32[7,50,128]{1,0,2:T(8,128)S(1)} %copy.207, f32[50,50,128]{1,0,2:T(8,128)} %copy.172), kind=kOutput, calls=%fused_computation.199 | convolution fusion | flops 26880000 | bytes 1638400 | tf_op jit(solution)/shard_map/klc,tkc->tlc/dot_general | solution.py:70
  85.7 0.2 copy.209
  86.0 0.3 convolution_bitcast_fusion.6
  86.3 0.9 convolution_bitcast_fusion.3
  87.2 0.6 convolution_bitcast_fusion
  87.8 0.4 copy.230
  88.2 0.1 slice_bitcast_fusion.3
  88.3 1.9 %collective-permute-start.8 = (f32[7,50,128]{2,0,1:T(8,128)S(1)}, f32[7,50,128]{2,0,1:T(8,128)S(1)}, u32[]{:S(2)}, u32[]{:S(2)}) collective-permute-start(f32[7,50,128]{2,0,1:T(8,128)S(1)} %get-tuple-element.26), channel_id=1, source_target_pairs={{0,1},{1,2},{2,3},{3,4},{4,5},{5,6},{6,7},{7,8},{8,9},{9,10},{10,1... | collective-permute-start | bytes 537608 | tf_op jit(solution)/shard_map/ppermute | solution.py:16
  90.2 8.8 %collective-permute-start.11 = (f32[7,50,128]{2,0,1:T(8,128)S(1)}, f32[7,50,128]{2,0,1:T(8,128)S(1)}, u32[]{:S(2)}, u32[]{:S(2)}) collective-permute-start(f32[7,50,128]{2,0,1:T(8,128)S(1)} %get-tuple-element.27), channel_id=1, source_target_pairs={{2,0},{3,1},{4,2},{5,3},{6,4},{7,5},{8,6},{9,7},{10,8},{11,9},{12,... | collective-permute-start | bytes 537608 | tf_op jit(solution)/shard_map/ppermute | solution.py:16
  99.1 1.9 %collective-permute-start.10 = (f32[7,50,128]{2,0,1:T(8,128)S(1)}, f32[7,50,128]{2,0,1:T(8,128)S(1)}, u32[]{:S(2)}, u32[]{:S(2)}) collective-permute-start(f32[7,50,128]{2,0,1:T(8,128)S(1)} %get-tuple-element.28), channel_id=1, source_target_pairs={{0,2},{1,3},{2,4},{3,5},{4,6},{5,7},{6,8},{7,9},{8,10},{9,11},{10,... | collective-permute-start | bytes 537608 | tf_op jit(solution)/shard_map/ppermute | solution.py:16
  101.0 2.4 %collective-permute-start.9 = (f32[7,50,128]{2,0,1:T(8,128)S(1)}, f32[7,50,128]{2,0,1:T(8,128)S(1)}, u32[]{:S(2)}, u32[]{:S(2)}) collective-permute-start(f32[7,50,128]{2,0,1:T(8,128)S(1)} %get-tuple-element.29), channel_id=1, source_target_pairs={{1,0},{2,1},{3,2},{4,3},{5,4},{6,5},{7,6},{8,7},{9,8},{10,9},{11,1... | collective-permute-start | bytes 537608 | tf_op jit(solution)/shard_map/ppermute | solution.py:16
  103.4 0.3 multiply_add_fusion.3
  103.8 0.2 multiply_add_fusion.6
  103.9 0.5 multiply_multiply_fusion
  104.4 0.1 multiply_add_fusion.1
  104.5 6.8 %collective-permute-done.10 = f32[7,50,128]{2,0,1:T(8,128)S(1)} collective-permute-done((f32[7,50,128]{2,0,1:T(8,128)S(1)}, f32[7,50,128]{2,0,1:T(8,128)S(1)}, u32[]{:S(2)}, u32[]{:S(2)}) %collective-permute-start.10) | collective-permute-done | bytes 179232 | tf_op jit(solution)/shard_map/ppermute | solution.py:16
  111.3 0.2 fusion.6
  111.6 0.7 copy.225
  (26 shorter events, 0.2 us)
Async XLA Ops:
  0.0 14.6 %copy-start = (bf16[30,128,128]{2,1,0:T(8,128)(2,1)S(1)}, bf16[30,128,128]{2,1,0:T(8,128)(2,1)}, u32[]{:S(2)}) copy-start(bf16[30,128,128]{2,1,0:T(8,128)(2,1)} %param.14) | copy-start | bytes 2949124
  8.7 5.6 %copy-start.6 = (s32[30]{0:T(128)S(1)}, s32[30]{0:T(128)}, u32[]{:S(2)}) copy-start(s32[30]{0:T(128)} %param.12) | copy-start | bytes 364
  16.6 23.6 %collective-permute-start = (f32[7,50,128]{2,0,1:T(8,128)S(1)}, f32[7,50,128]{2,0,1:T(8,128)S(1)}, u32[]{:S(2)}, u32[]{:S(2)}) collective-permute-start(f32[7,50,128]{2,0,1:T(8,128)S(1)} %get-tuple-element.34), channel_id=1, source_target_pairs={{0,1},{1,2},{2,3},{3,4},{4,5},{5,6},{6,7},{7,8},{8,9},{9,10},{10,1... | collective-permute-start | bytes 537608 | tf_op jit(solution)/shard_map/ppermute | solution.py:16
  20.4 19.8 %collective-permute-start.3 = (f32[7,50,128]{2,0,1:T(8,128)S(1)}, f32[7,50,128]{2,0,1:T(8,128)S(1)}, u32[]{:S(2)}, u32[]{:S(2)}) collective-permute-start(f32[7,50,128]{2,0,1:T(8,128)S(1)} %get-tuple-element.35), channel_id=1, source_target_pairs={{2,0},{3,1},{4,2},{5,3},{6,4},{7,5},{8,6},{9,7},{10,8},{11,9},{12,... | collective-permute-start | bytes 537608 | tf_op jit(solution)/shard_map/ppermute | solution.py:16
  32.4 11.7 %collective-permute-start.2 = (f32[7,50,128]{2,0,1:T(8,128)S(1)}, f32[7,50,128]{2,0,1:T(8,128)S(1)}, u32[]{:S(2)}, u32[]{:S(2)}) collective-permute-start(f32[7,50,128]{2,0,1:T(8,128)S(1)} %get-tuple-element.36), channel_id=1, source_target_pairs={{0,2},{1,3},{2,4},{3,5},{4,6},{5,7},{6,8},{7,9},{8,10},{9,11},{10,... | collective-permute-start | bytes 537608 | tf_op jit(solution)/shard_map/ppermute | solution.py:16
  34.3 9.8 %collective-permute-start.1 = (f32[7,50,128]{2,0,1:T(8,128)S(1)}, f32[7,50,128]{2,0,1:T(8,128)S(1)}, u32[]{:S(2)}, u32[]{:S(2)}) collective-permute-start(f32[7,50,128]{2,0,1:T(8,128)S(1)} %get-tuple-element.37), channel_id=1, source_target_pairs={{1,0},{2,1},{3,2},{4,3},{5,4},{6,5},{7,6},{8,7},{9,8},{10,9},{11,1... | collective-permute-start | bytes 537608 | tf_op jit(solution)/shard_map/ppermute | solution.py:16
  39.1 11.5 %copy-start.3 = (f32[1,1,50,128]{3,2,1,0:T(8,128)}, f32[1,1,50,128]{3,2,1,0:T(8,128)S(1)}, u32[]{:S(2)}) copy-start(f32[1,1,50,128]{3,2,1,0:T(8,128)S(1)} %get-tuple-element.44) | copy-start | bytes 76804
  52.3 0.6 copy-start.4
  55.6 17.9 %collective-permute-start.4 = (f32[7,50,128]{2,0,1:T(8,128)S(1)}, f32[7,50,128]{2,0,1:T(8,128)S(1)}, u32[]{:S(2)}, u32[]{:S(2)}) collective-permute-start(f32[7,50,128]{2,0,1:T(8,128)S(1)} %get-tuple-element.30), channel_id=1, source_target_pairs={{0,1},{1,2},{2,3},{3,4},{4,5},{5,6},{6,7},{7,8},{8,9},{9,10},{10,1... | collective-permute-start | bytes 537608 | tf_op jit(solution)/shard_map/ppermute | solution.py:16
  57.5 16.0 %collective-permute-start.7 = (f32[7,50,128]{2,0,1:T(8,128)S(1)}, f32[7,50,128]{2,0,1:T(8,128)S(1)}, u32[]{:S(2)}, u32[]{:S(2)}) collective-permute-start(f32[7,50,128]{2,0,1:T(8,128)S(1)} %get-tuple-element.31), channel_id=1, source_target_pairs={{2,0},{3,1},{4,2},{5,3},{6,4},{7,5},{8,6},{9,7},{10,8},{11,9},{12,... | collective-permute-start | bytes 537608 | tf_op jit(solution)/shard_map/ppermute | solution.py:16
  66.9 12.2 %collective-permute-start.6 = (f32[7,50,128]{2,0,1:T(8,128)S(1)}, f32[7,50,128]{2,0,1:T(8,128)S(1)}, u32[]{:S(2)}, u32[]{:S(2)}) collective-permute-start(f32[7,50,128]{2,0,1:T(8,128)S(1)} %get-tuple-element.32), channel_id=1, source_target_pairs={{0,2},{1,3},{2,4},{3,5},{4,6},{5,7},{6,8},{7,9},{8,10},{9,11},{10,... | collective-permute-start | bytes 537608 | tf_op jit(solution)/shard_map/ppermute | solution.py:16
  68.8 10.3 %collective-permute-start.5 = (f32[7,50,128]{2,0,1:T(8,128)S(1)}, f32[7,50,128]{2,0,1:T(8,128)S(1)}, u32[]{:S(2)}, u32[]{:S(2)}) collective-permute-start(f32[7,50,128]{2,0,1:T(8,128)S(1)} %get-tuple-element.33), channel_id=1, source_target_pairs={{1,0},{2,1},{3,2},{4,3},{5,4},{6,5},{7,6},{8,7},{9,8},{10,9},{11,1... | collective-permute-start | bytes 537608 | tf_op jit(solution)/shard_map/ppermute | solution.py:16
  85.7 17.7 %copy-start.2 = (f32[1,1,50,128]{3,2,1,0:T(8,128)S(1)}, f32[1,1,50,128]{3,2,1,0:T(8,128)}, u32[]{:S(2)}) copy-start(f32[1,1,50,128]{3,2,1,0:T(8,128)} %get-tuple-element.38) | copy-start | bytes 76804
  86.0 17.9 %copy-start.1 = (f32[1,1,50,128]{3,2,1,0:T(8,128)S(1)}, f32[1,1,50,128]{3,2,1,0:T(8,128)}, u32[]{:S(2)}) copy-start(f32[1,1,50,128]{3,2,1,0:T(8,128)} %get-tuple-element.39) | copy-start | bytes 76804
  86.0 18.4 %copy-start.5 = (f32[1,1,50,128]{3,2,1,0:T(8,128)S(1)}, f32[1,1,50,128]{3,2,1,0:T(8,128)}, u32[]{:S(2)}) copy-start(f32[1,1,50,128]{3,2,1,0:T(8,128)} %get-tuple-element.55) | copy-start | bytes 76804
  88.3 16.2 %collective-permute-start.8 = (f32[7,50,128]{2,0,1:T(8,128)S(1)}, f32[7,50,128]{2,0,1:T(8,128)S(1)}, u32[]{:S(2)}, u32[]{:S(2)}) collective-permute-start(f32[7,50,128]{2,0,1:T(8,128)S(1)} %get-tuple-element.26), channel_id=1, source_target_pairs={{0,1},{1,2},{2,3},{3,4},{4,5},{5,6},{6,7},{7,8},{8,9},{9,10},{10,1... | collective-permute-start | bytes 537608 | tf_op jit(solution)/shard_map/ppermute | solution.py:16
  90.2 14.3 %collective-permute-start.11 = (f32[7,50,128]{2,0,1:T(8,128)S(1)}, f32[7,50,128]{2,0,1:T(8,128)S(1)}, u32[]{:S(2)}, u32[]{:S(2)}) collective-permute-start(f32[7,50,128]{2,0,1:T(8,128)S(1)} %get-tuple-element.27), channel_id=1, source_target_pairs={{2,0},{3,1},{4,2},{5,3},{6,4},{7,5},{8,6},{9,7},{10,8},{11,9},{12,... | collective-permute-start | bytes 537608 | tf_op jit(solution)/shard_map/ppermute | solution.py:16
  99.1 12.2 %collective-permute-start.10 = (f32[7,50,128]{2,0,1:T(8,128)S(1)}, f32[7,50,128]{2,0,1:T(8,128)S(1)}, u32[]{:S(2)}, u32[]{:S(2)}) collective-permute-start(f32[7,50,128]{2,0,1:T(8,128)S(1)} %get-tuple-element.28), channel_id=1, source_target_pairs={{0,2},{1,3},{2,4},{3,5},{4,6},{5,7},{6,8},{7,9},{8,10},{9,11},{10,... | collective-permute-start | bytes 537608 | tf_op jit(solution)/shard_map/ppermute | solution.py:16
  101.0 10.3 %collective-permute-start.9 = (f32[7,50,128]{2,0,1:T(8,128)S(1)}, f32[7,50,128]{2,0,1:T(8,128)S(1)}, u32[]{:S(2)}, u32[]{:S(2)}) collective-permute-start(f32[7,50,128]{2,0,1:T(8,128)S(1)} %get-tuple-element.29), channel_id=1, source_target_pairs={{1,0},{2,1},{3,2},{4,3},{5,4},{6,5},{7,6},{8,7},{9,8},{10,9},{11,1... | collective-permute-start | bytes 537608 | tf_op jit(solution)/shard_map/ppermute | solution.py:16
where the time goes:
time: 114 us; the launch traced here: 112 us
  starting transfers between devices  51.6 us (45%)
  matrix products  21.1 us (19%)
  waiting for transfers between devices  16.3 us (14%)
  other arithmetic  11.3 us (10%)
  local copies, waits for them, and re-layouts  10.7 us (9%)
  between operations  1.16 us (1%)
    ppermute x12, starting transfers between devices, shifted(): return lax.ppermute(value, axis, pairs)  51.6 us
    ppermute x12, waiting for transfers between devices, shifted(): return lax.ppermute(value, axis, pairs)  16.3 us
    dot_general x3, matrix products, shards(): jnp.einsum('klc,tkc->tlc', implicit, adjoint, precision=highest) * wet_mask  15.9 us
    unnamed x16, local copies, waits for them, and re-layouts  7.27 us
    dot_general x3, matrix products, shards(): terms = jnp.einsum('tsi,sij->tsj', picked, wide_tiles, precision=highest)  2.64 us
  transfers between devices with their start and end apart: 12, of which 3 were waited for; matrix products, arithmetic and copies ran while one was open for 5% of the time, Pallas kernels for 0%

commit v1 on v0

v1 whole, which is shorter than its diff:
```python
import functools
import jax
import jax.numpy as jnp
from jax import lax
from jax.experimental import pallas as pl
from jax.experimental.pallas import tpu as pltpu
from jax.sharding import PartitionSpec as P

STEPS = 3
TRC = 7
LEV = 50
PAD = 56
SLOTS = 30
REACH = 2
KEYS = 2 * REACH + 1
time_step = 0.5
BLK, ROW, SLOT, START = 0, 32, 64, 96


def pull_back(states, carried, light):
    phosphate, _, oxygen, plankton, grazers, detritus, nitrate = states
    c_pho, c_dis, c_oxy, c_pla, c_gra, c_det, c_nit = carried
    rp = 1.0 / (0.03 + phosphate)
    rn = 1.0 / (0.5 + nitrate)
    ro = 1.0 / (1.0 + oxygen)
    p2 = plankton * plankton
    rg = 1.0 / (0.1 + p2)
    mix = c_pho - 1.2 * c_oxy + 1.6 * c_nit
    a_growth = 0.1 * c_dis + c_pla - mix
    a_grazing = 0.3 * c_pho - c_pla + 0.7 * c_gra
    a_mortality = 0.1 * c_dis - c_pla + 0.9 * c_det
    a_remineral = mix - c_det
    a_decay = mix - c_dis
    a_loss = c_det - c_gra
    fp = phosphate * rp
    fn = nitrate * rn
    lg = (1.2 * light) * a_growth
    lgp = lg * plankton
    d_pho = lgp * fn * (0.03 * rp * rp)
    d_nit = lgp * fp * (0.5 * rn * rn)
    hol = p2 * rg
    ag = 1.9 * a_grazing
    d_pla = lg * fp * fn + ag * grazers * (0.2 * plankton * rg * rg) + 0.06 * plankton * a_mortality
    d_gra = ag * hol + 0.1 * grazers * a_loss
    ar = 0.05 * a_remineral
    d_det = ar * oxygen * ro
    d_oxy = ar * detritus * (ro * ro)
    d_dis = 0.17 * a_decay
    return [d_pho, d_dis, d_oxy, d_pla, d_gra, d_det, d_nit]


def advance(adj_ref, implicit_ref, states_ref, wet, base_ref, planes):
    level_ids = lax.broadcasted_iota(jnp.int32, (LEV, 128), 0)
    mask = (level_ids < wet).astype(jnp.float32)
    light = jnp.exp(-0.2 * level_ids.astype(jnp.float32))

    def term(k, acc):
        m = implicit_ref[k]
        return tuple(acc[t] + m * adj_ref[t, pl.ds(k, 1), :] for t in range(TRC))

    acc = tuple(jnp.zeros((LEV, 128), jnp.float32) for _ in range(TRC))
    acc = lax.fori_loop(0, LEV, term, acc, unroll=5)
    carried = [a * mask for a in acc]
    for t in range(TRC):
        planes[pl.ds(t, LEV, stride=8), :] = carried[t]
    bio = pull_back([states_ref[t] for t in range(TRC)], carried, light)
    for t in range(TRC):
        base_ref[t] = carried[t] + time_step * bio[t]


def make_terms(planes, tiles_ref, slot_of, row_of, out_ref):
    for p in range(SLOTS):
        row = pl.multiple_of(row_of(p) * 8, 8)
        picked = planes[pl.ds(row, 8), :]
        hi = picked.astype(jnp.bfloat16)
        lo = (picked - hi.astype(jnp.float32)).astype(jnp.bfloat16)
        both = jnp.concatenate([hi, lo], axis=0)
        prod = jnp.dot(both, tiles_ref[slot_of(p)], preferred_element_type=jnp.float32)
        out_ref[p] = prod[:8] + prod[8:]


def first_kernel(rows, cols, count, wet_ref, final_ref, implicit_ref, states_ref, tiles_ref,
                 out_ref, base_ref, planes, order, starts):
    me = lax.axis_index("col")
    live = count[0]
    origin = (me - REACH) * LEV

    def key_of(s):
        r = cols[s] - origin
        return sum((r >= LEV * j).astype(jnp.int32) for j in range(1, KEYS)), r

    for j in range(8):
        starts[j] = 0

    def tally(s, carry):
        key, _ = key_of(s)
        starts[key + 1] = starts[key + 1] + 1
        return carry

    lax.fori_loop(0, live, tally, 0)
    for j in range(1, 7):
        starts[j] = starts[j] + starts[j - 1]
    lane = lax.broadcasted_iota(jnp.int32, (1, 128), 1)
    info = jnp.zeros((1, 128), jnp.int32)
    for j in range(KEYS + 1):
        info = jnp.where(lane == START + j, starts[j], info)
    for p in range(3 * 32):
        order[p] = 0

    def place(s, carry):
        key, r = key_of(s)
        p = starts[key]
        starts[key] = p + 1
        order[BLK + p] = r - LEV * key
        order[ROW + p] = rows[s] - me * LEV
        order[SLOT + p] = s
        return carry

    lax.fori_loop(0, live, place, 0)
    for p in range(SLOTS):
        for base in (BLK, ROW, SLOT):
            info = jnp.where(lane == base + p, order[base + p], info)

    planes[...] = jnp.zeros_like(planes)
    advance(final_ref, implicit_ref, states_ref, wet_ref[...], base_ref, planes)
    make_terms(planes, tiles_ref, lambda p: order[SLOT + p], lambda p: order[ROW + p], out_ref)
    out_ref[0, 7:8, :] = info.astype(jnp.float32)


def receive(got_ref, info_v, info_s, planes, sem):
    me = lax.axis_index("col")
    core = lax.rem(me, 2)
    chip = lax.div(me, 2)
    odd = lax.rem(chip, 2)
    even_chip = chip + 1 - 2 * odd
    odd_chip = chip - 1 + 2 * odd
    places = []
    for k in range(2):
        places.append((2 * odd + k, 2 * chip + k))
        places.append((2 * (1 - odd) + k, 2 * even_chip + k))
        places.append((4 + 2 * odd + k, 2 * odd_chip + k))
    for i, (chunk, _) in enumerate(places):
        info_v[i : i + 1, :] = got_ref[chunk * SLOTS, 7:8, :].astype(jnp.int32)
    copy = pltpu.make_async_copy(info_v, info_s, sem)
    copy.start()
    planes[...] = jnp.zeros_like(planes)
    copy.wait()
    for i, (chunk, src) in enumerate(places):
        key = me - src + REACH
        inside = (key >= 0) & (key < KEYS)
        safe = jnp.clip(key, 0, KEYS - 1)
        begin = info_s[i, START + safe]
        end = jnp.where(inside, info_s[i, START + safe + 1], begin)

        def add(p, carry, i=i, chunk=chunk):
            at = pl.multiple_of(info_s[i, BLK + p] * 8, 8)
            planes[pl.ds(at, 8), :] = planes[pl.ds(at, 8), :] + got_ref[chunk * SLOTS + p]
            return carry

        lax.fori_loop(begin, end, add, 0)
    return jnp.where(core == 0, 0, 3)


def gather_adjoint(planes, base_ref, wet, out_ref):
    level_ids = lax.broadcasted_iota(jnp.int32, (LEV, 128), 0)
    mask = (level_ids < wet).astype(jnp.float32)
    for t in range(TRC):
        out_ref[t] = mask * (base_ref[t] + planes[pl.ds(t, LEV, stride=8), :])


def next_kernel(got_ref, wet_ref, base_in, implicit_ref, states_ref, tiles_ref, out_ref, base_ref,
                planes, adj, info_v, info_s, sem):
    own = receive(got_ref, info_v, info_s, planes, sem)
    gather_adjoint(planes, base_in, wet_ref[...], adj)
    planes[...] = jnp.zeros_like(planes)
    advance(adj, implicit_ref, states_ref, wet_ref[...], base_ref, planes)
    make_terms(planes, tiles_ref, lambda p: info_s[own, SLOT + p], lambda p: info_s[own, ROW + p], out_ref)
    out_ref[0, 7:8, :] = info_v[pl.ds(own, 1), :].astype(jnp.float32)


def last_kernel(got_ref, wet_ref, base_in, out_ref, planes, info_v, info_s, sem):
    receive(got_ref, info_v, info_s, planes, sem)
    gather_adjoint(planes, base_in, wet_ref[...], out_ref)


VMEM = pl.BlockSpec(memory_space=pltpu.VMEM)
SMEM = pl.BlockSpec(memory_space=pltpu.SMEM)
f32 = jnp.float32
PARAMS = pltpu.CompilerParams(vmem_limit_bytes=24 * 1024 * 1024)


def shards(final_adjoint, states, implicit, wet_levels, tile_rows, tile_cols, tiles, tile_count):
    devices = lax.axis_size("col")
    inside = [[2 * c, 2 * c + 1] for c in range(devices // 2)]
    across = [[2 * c, 2 * c + 2] for c in range(0, devices // 2, 2)]
    across += [[2 * c + 1, (2 * c + 3) % devices] for c in range(1, devices // 2, 2)]
    wet = wet_levels.reshape(1, 128)
    slots = jax.ShapeDtypeStruct((SLOTS, 8, 128), f32)
    field = jax.ShapeDtypeStruct((TRC, LEV, 128), f32)
    planes = pltpu.VMEM((PAD * 8, 128), f32)
    infos = [pltpu.VMEM((8, 128), jnp.int32), pltpu.SMEM((8, 128), jnp.int32), pltpu.SemaphoreType.DMA]

    def exchange(terms):
        for groups in (inside, across, inside):
            terms = lax.all_gather(terms, "col", axis_index_groups=groups, tiled=True)
        return terms

    terms, base = pl.pallas_call(
        first_kernel,
        in_specs=[SMEM] * 3 + [VMEM] * 5,
        out_specs=[VMEM] * 2,
        out_shape=[slots, field],
        scratch_shapes=[planes, pltpu.SMEM((96,), jnp.int32), pltpu.SMEM((8,), jnp.int32)],
        compiler_params=PARAMS,
    )(tile_rows, tile_cols, tile_count, wet, final_adjoint, implicit, states[STEPS - 1], tiles)
    for section in range(STEPS - 2, -1, -1):
        got = exchange(terms)
        terms, base = pl.pallas_call(
            next_kernel,
            in_specs=[VMEM] * 6,
            out_specs=[VMEM] * 2,
            out_shape=[slots, field],
            scratch_shapes=[planes, pltpu.VMEM((TRC, LEV, 128), f32)] + infos,
            compiler_params=PARAMS,
        )(got, wet, base, implicit, states[section], tiles)
    got = exchange(terms)
    return pl.pallas_call(
        last_kernel,
        in_specs=[VMEM] * 3,
        out_specs=VMEM,
        out_shape=field,
        scratch_shapes=[planes] + infos,
        compiler_params=PARAMS,
    )(got, wet, base)


def solution(mesh):
    in_specs = (
        P(None, None, "col"),
        P(None, None, None, "col"),
        P(None, None, "col"),
        P("col"),
        P("col"),
        P("col"),
        P("col", None, None),
        P("col"),
    )
    out_specs = P(None, None, "col")
    return jax.shard_map(shards, mesh=mesh, in_specs=in_specs, out_specs=out_specs, check_vma=False)
```

time: 114 us -> 70.5 us (0.62)
  the two profiles are of different devices: /device:TPU:7 before, /device:TPU:1 now
where the time goes in v1:
time: 70.5 us; the launch traced here: 70.2 us
  blocking collectives  56 us (79%)
  Pallas kernels  7.98 us (11%)
  local copies, waits for them, and re-layouts  5.42 us (8%)
  between operations  0.8 us (1%)
    all_gather x9, blocking collectives, exchange(): terms = lax.all_gather(terms, 'col', axis_index_groups=groups, tiled=True)  56 us
    pallas_call x2, Pallas kernels, shards(): pl.pallas_call(next_kernel, in_specs=[VMEM] * 6, out_specs=[VMEM] * 2, ou...  4.29 us
    unnamed x16, local copies, waits for them, and re-layouts  4.26 us
    pallas_call x1, Pallas kernels, shards(): pl.pallas_call(first_kernel, in_specs=[SMEM] * 3 + [VMEM] * 5, out_specs=...  2.18 us
    pallas_call x1, Pallas kernels, shards(): pl.pallas_call(last_kernel, in_specs=[VMEM] * 3, out_specs=VMEM, out_shap...  1.51 us

profile of v1, /device:TPU:1, one launch (start us, length us, event | category | flops | bytes accessed | tf_op | source)
XLA Modules:
  0.0 70.2 jit_solution(5068189102336641106)
XLA Ops:
  0.0 0.0 copy-start.2
  0.7 1.2 %slice_bitcast_fusion = (f32[7,50,128]{2,1,0:T(8,128)S(1)}, f32[7,50,128]{2,1,0:T(8,128)S(1)}, f32[7,50,128]{2,1,0:T(8,128)S(1)}) fusion(f32[3,7,50,128]{3,2,1,0:T(8,128)} %param.9), kind=kLoop, calls=%fused_computation | loop fusion | bytes 1075200 | tf_op jit(solution)/shard_map/squeeze | solution.py:225
  1.9 0.0 copy-done.2
  1.9 0.0 copy-start
  1.9 1.4 %copy-done = f32[50,50,128]{2,1,0:T(8,128)S(1)} copy-done((f32[50,50,128]{2,1,0:T(8,128)S(1)}, f32[50,50,128]{2,1,0:T(8,128)}, u32[]{:S(2)}) %copy-start) | copy-done | bytes 1280024
  3.3 0.0 copy-start.3
  3.3 0.9 %copy-done.3 = f32[7,50,128]{2,1,0:T(8,128)S(1)} copy-done((f32[7,50,128]{2,1,0:T(8,128)S(1)}, f32[7,50,128]{2,1,0:T(8,128)}, u32[]{:S(2)}) %copy-start.3) | copy-done | bytes 179224
  4.2 0.0 copy-start.4
  4.2 0.7 copy-done.4
  4.9 0.0 copy-start.6
  4.9 0.7 copy-done.6
  5.5 0.0 copy-start.7
  5.5 0.7 copy-done.7
  6.2 2.2 %shard_map.82 = (f32[30,8,128]{2,1,0:T(8,128)S(1)}, f32[7,50,128]{2,1,0:T(8,128)S(1)}) custom-call(s32[30]{0:T(128)S(1)} %copy-done.6, s32[30]{0:T(128)S(1)} %copy-done.7, s32[1]{0:T(128)S(6)} %copy.9.count, s32[1,128]{1,0:T(1,128)S(1)} %bitcast.7, f32[7,50,128]{2,1,0:T(8,128)S(1)} %copy-done.3, f32[50,50,128]{2,1,0:T(8,128)S(1)} %copy-done, ...), custom_call_target="tpu_custom_call" | custom-call | tf_op jit(solution)/shard_map/pallas_call | solution.py:208
  8.4 0.0 copy-start.1
  8.4 8.5 %all_gather.27 = f32[60,8,128]{2,1,0:T(8,128)S(1)} all-gather(f32[30,8,128]{2,1,0:T(8,128)S(1)} %get-tuple-element.11), channel_id=1, replica_groups={{0,1},{2,3},{4,5},{6,7},{8,9},{10,11},{12,13},{14,15},{16,17},{18,19},{..., dimensions={0}, use_global_device_ids=true | all-gather | bytes 368640 | tf_op jit(solution)/shard_map/all_gather | solution.py:205
  16.9 13.5 %all_gather.28 = f32[120,8,128]{2,1,0:T(8,128)S(1)} all-gather(f32[60,8,128]{2,1,0:T(8,128)S(1)} %all_gather.27), channel_id=1, replica_groups={{0,2},{4,6},{8,10},{12,14},{16,18},{20,22},{24,26},{28,30},{32,34},{36,..., dimensions={0}, use_global_device_ids=true | all-gather | bytes 737280 | tf_op jit(solution)/shard_map/all_gather | solution.py:205
  30.4 2.5 %all_gather.29.got_ref = f32[240,8,128]{2,1,0:T(8,128)S(1)} all-gather(f32[120,8,128]{2,1,0:T(8,128)S(1)} %all_gather.28), channel_id=1, replica_groups={{0,1},{2,3},{4,5},{6,7},{8,9},{10,11},{12,13},{14,15},{16,17},{18,19},{..., dimensions={0}, use_global_device_ids=true | all-gather | bytes 1474560 | tf_op jit(solution)/shard_map/all_gather | solution.py:205
  32.9 0.0 copy-done.1
  32.9 2.1 %shard_map.83 = (f32[30,8,128]{2,1,0:T(8,128)S(1)}, f32[7,50,128]{2,1,0:T(8,128)S(1)}) custom-call(f32[240,8,128]{2,1,0:T(8,128)S(1)} %all_gather.29.got_ref, s32[1,128]{1,0:T(1,128)S(1)} %bitcast.8, f32[7,50,128]{2,1,0:T(8,128)S(1)} %get-tuple-element.12.base_in, f32[50,50,128]{2,1,0:T(8,128)S(1)} %copy-done.1, ...), custom_call_target="tpu_custom_call" | custom-call | tf_op jit(solution)/shard_map/pallas_call | solution.py:218
  35.0 0.0 copy-start.5
  35.0 2.0 %all_gather.30 = f32[60,8,128]{2,1,0:T(8,128)S(1)} all-gather(f32[30,8,128]{2,1,0:T(8,128)S(1)} %get-tuple-element.13), channel_id=1, replica_groups={{0,1},{2,3},{4,5},{6,7},{8,9},{10,11},{12,13},{14,15},{16,17},{18,19},{..., dimensions={0}, use_global_device_ids=true | all-gather | bytes 368640 | tf_op jit(solution)/shard_map/all_gather | solution.py:205
  37.0 11.3 %all_gather.31 = f32[120,8,128]{2,1,0:T(8,128)S(1)} all-gather(f32[60,8,128]{2,1,0:T(8,128)S(1)} %all_gather.30), channel_id=1, replica_groups={{0,2},{4,6},{8,10},{12,14},{16,18},{20,22},{24,26},{28,30},{32,34},{36,..., dimensions={0}, use_global_device_ids=true | all-gather | bytes 737280 | tf_op jit(solution)/shard_map/all_gather | solution.py:205
  48.3 2.5 %all_gather.32.got_ref = f32[240,8,128]{2,1,0:T(8,128)S(1)} all-gather(f32[120,8,128]{2,1,0:T(8,128)S(1)} %all_gather.31), channel_id=1, replica_groups={{0,1},{2,3},{4,5},{6,7},{8,9},{10,11},{12,13},{14,15},{16,17},{18,19},{..., dimensions={0}, use_global_device_ids=true | all-gather | bytes 1474560 | tf_op jit(solution)/shard_map/all_gather | solution.py:205
  50.8 0.0 copy-done.5
  50.8 2.1 %shard_map.84 = (f32[30,8,128]{2,1,0:T(8,128)S(1)}, f32[7,50,128]{2,1,0:T(8,128)S(1)}) custom-call(f32[240,8,128]{2,1,0:T(8,128)S(1)} %all_gather.32.got_ref, s32[1,128]{1,0:T(1,128)S(1)} %bitcast.9, f32[7,50,128]{2,1,0:T(8,128)S(1)} %get-tuple-element.14.base_in, f32[50,50,128]{2,1,0:T(8,128)S(1)} %copy-done.1, ...), custom_call_target="tpu_custom_call" | custom-call | tf_op jit(solution)/shard_map/pallas_call | solution.py:218
  53.0 2.0 %all_gather.33 = f32[60,8,128]{2,1,0:T(8,128)S(1)} all-gather(f32[30,8,128]{2,1,0:T(8,128)S(1)} %get-tuple-element.15), channel_id=1, replica_groups={{0,1},{2,3},{4,5},{6,7},{8,9},{10,11},{12,13},{14,15},{16,17},{18,19},{..., dimensions={0}, use_global_device_ids=true | all-gather | bytes 368640 | tf_op jit(solution)/shard_map/all_gather | solution.py:205
  54.9 11.3 %all_gather.34 = f32[120,8,128]{2,1,0:T(8,128)S(1)} all-gather(f32[60,8,128]{2,1,0:T(8,128)S(1)} %all_gather.33), channel_id=1, replica_groups={{0,2},{4,6},{8,10},{12,14},{16,18},{20,22},{24,26},{28,30},{32,34},{36,..., dimensions={0}, use_global_device_ids=true | all-gather | bytes 737280 | tf_op jit(solution)/shard_map/all_gather | solution.py:205
  66.2 2.5 %all_gather.35.got_ref = f32[240,8,128]{2,1,0:T(8,128)S(1)} all-gather(f32[120,8,128]{2,1,0:T(8,128)S(1)} %all_gather.34), channel_id=1, replica_groups={{0,1},{2,3},{4,5},{6,7},{8,9},{10,11},{12,13},{14,15},{16,17},{18,19},{..., dimensions={0}, use_global_device_ids=true | all-gather | bytes 1474560 | tf_op jit(solution)/shard_map/all_gather | solution.py:205
  68.7 1.5 %shard_map.85 = f32[7,50,128]{2,1,0:T(8,128)} custom-call(f32[240,8,128]{2,1,0:T(8,128)S(1)} %all_gather.35.got_ref, s32[1,128]{1,0:T(1,128)S(1)} %bitcast.10, f32[7,50,128]{2,1,0:T(8,128)S(1)} %get-tuple-element.16.base_in), custom_call_target="tpu_custom_call" | custom-call | tf_op jit(solution)/shard_map/pallas_call | solution.py:227
Async XLA Ops:
  0.0 1.9 %copy-start.2 = (bf16[30,128,128]{2,1,0:T(8,128)(2,1)S(1)}, bf16[30,128,128]{2,1,0:T(8,128)(2,1)}, u32[]{:S(2)}) copy-start(bf16[30,128,128]{2,1,0:T(8,128)(2,1)} %tiles_ref.5) | copy-start | bytes 2949124
  1.9 1.4 %copy-start = (f32[50,50,128]{2,1,0:T(8,128)S(1)}, f32[50,50,128]{2,1,0:T(8,128)}, u32[]{:S(2)}) copy-start(f32[50,50,128]{2,1,0:T(8,128)} %implicit_ref.5) | copy-start | bytes 3840004
  3.3 0.9 %copy-start.3 = (f32[7,50,128]{2,1,0:T(8,128)S(1)}, f32[7,50,128]{2,1,0:T(8,128)}, u32[]{:S(2)}) copy-start(f32[7,50,128]{2,1,0:T(8,128)} %final_ref.1) | copy-start | bytes 537604
  4.2 0.7 copy-start.4
  4.9 0.7 copy-start.6
  5.5 0.7 copy-start.7
  8.4 24.5 %copy-start.1 = (f32[50,50,128]{2,1,0:T(8,128)S(1)}, f32[50,50,128]{2,1,0:T(8,128)}, u32[]{:S(2)}) copy-start(f32[50,50,128]{2,1,0:T(8,128)} %implicit_ref.5) | copy-start | bytes 3840004
  35.0 15.8 %copy-start.5 = (s32[128]{0:T(128)S(1)}, s32[128]{0:T(128)}, u32[]{:S(2)}) copy-start(s32[128]{0:T(128)} %param.11) | copy-start | bytes 1540

commit v2 on v1

v2 whole, which is shorter than its diff:
```python
import functools
import jax
import jax.numpy as jnp
from jax import lax
from jax.experimental import pallas as pl
from jax.experimental.pallas import tpu as pltpu
from jax.sharding import PartitionSpec as P

STEPS = 3
TRC = 7
LEV = 50
PAD = 56
SLOTS = 30
REACH = 2
KEYS = 2 * REACH + 1
time_step = 0.5
SPAN = 32
INFO = SLOTS
CHUNK = TRC * SPAN
KEY = 64
NONE = -1000.0


def pull_back(states, carried, light):
    phosphate, _, oxygen, plankton, grazers, detritus, nitrate = states
    c_pho, c_dis, c_oxy, c_pla, c_gra, c_det, c_nit = carried
    rp = 1.0 / (0.03 + phosphate)
    rn = 1.0 / (0.5 + nitrate)
    ro = 1.0 / (1.0 + oxygen)
    p2 = plankton * plankton
    rg = 1.0 / (0.1 + p2)
    mix = c_pho - 1.2 * c_oxy + 1.6 * c_nit
    a_growth = 0.1 * c_dis + c_pla - mix
    a_grazing = 0.3 * c_pho - c_pla + 0.7 * c_gra
    a_mortality = 0.1 * c_dis - c_pla + 0.9 * c_det
    a_remineral = mix - c_det
    a_decay = mix - c_dis
    a_loss = c_det - c_gra
    fp = phosphate * rp
    fn = nitrate * rn
    lg = (1.2 * light) * a_growth
    lgp = lg * plankton
    d_pho = lgp * fn * (0.03 * rp * rp)
    d_nit = lgp * fp * (0.5 * rn * rn)
    hol = p2 * rg
    ag = 1.9 * a_grazing
    d_pla = lg * fp * fn + ag * grazers * (0.2 * plankton * rg * rg) + 0.06 * plankton * a_mortality
    d_gra = ag * hol + 0.1 * grazers * a_loss
    ar = 0.05 * a_remineral
    d_det = ar * oxygen * ro
    d_oxy = ar * detritus * (ro * ro)
    d_dis = 0.17 * a_decay
    return [d_pho, d_dis, d_oxy, d_pla, d_gra, d_det, d_nit]


def wet_mask(wet):
    level_ids = lax.broadcasted_iota(jnp.int32, (LEV, 128), 0)
    return (level_ids < wet).astype(jnp.float32)


def advance(adj_ref, implicit_ref, wet, carried_ref, planes, arrive=None, parts=1):
    def term(k, acc):
        m = implicit_ref[k]
        return tuple(acc[t] + m * adj_ref[t, pl.ds(k, 1), :] for t in range(TRC))

    acc = tuple(jnp.zeros((LEV, 128), jnp.float32) for _ in range(TRC))
    for part in range(parts):
        if arrive is not None:
            arrive(part)
        acc = lax.fori_loop(part * LEV // parts, (part + 1) * LEV // parts, term, acc, unroll=25)
    mask = wet_mask(wet)
    for t in range(TRC):
        carried = acc[t] * mask
        planes[pl.ds(t, LEV, stride=8), :] = carried
        carried_ref[t] = carried


def make_terms(planes, tiles_ref, rows, out_ref):
    origin = lax.axis_index("col") * LEV
    for t in range(TRC):
        out_ref[t * SPAN + 24 : (t + 1) * SPAN, :] = jnp.zeros((8, 128), jnp.float32)
    for p in range(SLOTS):
        row = pl.multiple_of(jnp.clip(rows[p] - origin, 0, LEV - 1) * 8, 8)
        picked = planes[pl.ds(row, 8), :]
        hi = picked.astype(jnp.bfloat16)
        lo = (picked - hi.astype(jnp.float32)).astype(jnp.bfloat16)
        both = jnp.concatenate([hi, lo], axis=0)
        prod = jnp.dot(both, tiles_ref[p], preferred_element_type=jnp.float32)
        out_ref[pl.ds(p, TRC, stride=SPAN), :] = prod[:TRC] + prod[8 : 8 + TRC]


def first_kernel(rows_h, cols_h, count_h, wet_h, final_h, implicit_h, tiles_h,
                 out_ref, carried_ref, wet, implicit, tiles, adj, planes, rows, cols, count, sems):
    used = [0]

    def begin(src, dst):
        copy = pltpu.make_async_copy(src, dst, sems.at[used[0]])
        used[0] += 1
        copy.start()
        return copy

    span = LEV // PARTS
    small = [begin(final_h, adj), begin(wet_h, wet)]
    parts = [begin(implicit_h.at[pl.ds(i * span, span)], implicit.at[pl.ds(i * span, span)]) for i in range(PARTS)]
    small += [begin(cols_h, cols), begin(count_h, count), begin(rows_h, rows)]
    half = SLOTS // 2
    late = [begin(tiles_h.at[pl.ds(i * half, half)], tiles.at[pl.ds(i * half, half)]) for i in range(2)]
    for copy in small[:2]:
        copy.wait()
    advance(adj, implicit, wet[...], carried_ref, planes, lambda i: parts[i].wait(), PARTS)
    for copy in small[2:] + late:
        copy.wait()
    make_terms(planes, tiles, rows, out_ref)
    place = cols[...] - (lax.axis_index("col") - REACH) * LEV
    key = sum((place >= LEV * j).astype(jnp.int32) for j in range(1, KEYS))
    lane = lax.broadcasted_iota(jnp.int32, (1, SLOTS), 1)
    code = jnp.where(lane < count[0], place + (KEY - LEV) * key, -1).astype(jnp.float32)
    out_ref[INFO : INFO + 1, :] = jnp.full((1, 128), -1.0, jnp.float32)
    for i in range(128 // SPAN):
        out_ref[INFO : INFO + 1, i * SPAN : i * SPAN + SLOTS] = code


def origins(split):
    me = lax.axis_index("col")
    chip = lax.div(me, 2)
    odd = lax.rem(chip, 2)
    if split:
        chips = [chip, chip + 1 - 2 * odd, chip - 1 + 2 * odd]
    else:
        even_edge = chip - odd
        odd_edge = chip - 1 + odd
        away = -(2 ** 20)
        chips = [even_edge, even_edge + 1, jnp.where(odd == 1, away, odd_edge), jnp.where(odd == 1, odd_edge + 1, away)]
    return [2 * c + k for c in chips for k in range(2)]


def receive(chunks, split, take):
    me = lax.axis_index("col")
    lane = lax.broadcasted_iota(jnp.int32, (1, 128), 1)
    level = lax.broadcasted_iota(jnp.int32, (64, 128), 0).astype(jnp.float32)
    bases = [jnp.where(src < -REACH, -100, me - src + REACH) * KEY for src in origins(split)]
    per = 128 // SPAN
    marks = []
    for first in range(0, len(chunks), per):
        number = min(per, len(chunks) - first)
        codes = jnp.full((1, 128), NONE, jnp.float32)
        for i in range(number):
            here = (lane >= i * SPAN) & (lane < (i + 1) * SPAN)
            ref, at = chunks[first + i]
            found = ref[at + INFO : at + INFO + 1, :] - bases[first + i].astype(jnp.float32)
            codes = jnp.where(here, found, codes)
        marks.append((level == codes).astype(jnp.float32).astype(jnp.bfloat16)[:, : number * SPAN])
    marks = jnp.concatenate(marks, axis=1)
    for t in range(TRC):
        data = jnp.concatenate([ref[at + t * SPAN : at + (t + 1) * SPAN, :] for ref, at in chunks], axis=0)
        hi = data.astype(jnp.bfloat16)
        lo = (data - hi.astype(jnp.float32)).astype(jnp.bfloat16)
        both = jnp.dot(marks, jnp.concatenate([hi, lo], axis=1), preferred_element_type=jnp.float32)
        take(t, both[:LEV, :128] + both[:LEV, 128:])


def chunks_of(gots):
    return [(ref, at) for ref in gots for at in range(0, ref.shape[0], CHUNK)]


def local_part(carried_ref, states_ref, section, base):
    level_ids = lax.broadcasted_iota(jnp.int32, (LEV, 128), 0)
    light = jnp.exp(-0.2 * level_ids.astype(jnp.float32))
    carried = [carried_ref[t] for t in range(TRC)]
    bio = pull_back([states_ref[section, t] for t in range(TRC)], carried, light)
    for t in range(TRC):
        base[t] = carried[t] + time_step * bio[t]


def adjoint_into(out_ref, gots, wet_ref, base):
    mask = wet_mask(wet_ref[...])

    def take(t, transport):
        out_ref[t] = mask * (base[t] + transport)

    receive(chunks_of(gots), len(gots) == 2, take)


def next_kernel(section, number, *refs):
    gots, refs = refs[:number], refs[number:]
    (rows_h, wet_ref, carried_in, implicit_ref, states_ref, tiles_ref,
     out_ref, carried_ref, base, planes, adj, rows, sem) = refs
    copy = pltpu.make_async_copy(rows_h, rows, sem)
    copy.start()
    local_part(carried_in, states_ref, section + 1, base)
    adjoint_into(adj, gots, wet_ref, base)
    advance(adj, implicit_ref, wet_ref[...], carried_ref, planes)
    copy.wait()
    make_terms(planes, tiles_ref, rows, out_ref)
    me = lax.axis_index("col")
    core = lax.rem(me, 2)
    own = core if number == 2 else 2 * lax.rem(lax.div(me, 2), 2) + core
    out_ref[INFO : INFO + 1, :] = gots[0][pl.ds(own * CHUNK + INFO, 1), :]


def last_kernel(*refs):
    gots, (wet_ref, carried_in, states_ref, out_ref, base) = refs[:-5], refs[-5:]
    local_part(carried_in, states_ref, 0, base)
    adjoint_into(out_ref, gots, wet_ref, base)


VMEM = pl.BlockSpec(memory_space=pltpu.VMEM)
HBM = pl.BlockSpec(memory_space=pltpu.HBM)
f32 = jnp.float32
PARTS = 2
SWAP_STEP = 1
MIB = 1024 * 1024


def shards(final_adjoint, states, implicit, wet_levels, tile_rows, tile_cols, tiles, tile_count):
    devices = lax.axis_size("col")
    inside = [[2 * c, 2 * c + 1] for c in range(devices // 2)]
    across = [[2 * c, 2 * c + 2] for c in range(0, devices // 2, 2)]
    across += [[2 * c + 1, (2 * c + 3) % devices] for c in range(1, devices // 2, 2)]
    swaps = [pair for a, b in across[:-1] for pair in ((a, b), (b, a))]
    slots = jax.ShapeDtypeStruct((CHUNK, 128), f32)
    field = jax.ShapeDtypeStruct((TRC, LEV, 128), f32)
    scratch = pltpu.VMEM((TRC, LEV, 128), f32)
    planes = pltpu.VMEM((PAD * 8, 128), f32)
    rows = pltpu.SMEM((SLOTS,), jnp.int32)
    wet = wet_levels.reshape(1, 128)

    def gather(x, groups):
        return lax.all_gather(x, "col", axis_index_groups=groups, tiled=True)

    def exchange(terms, step):
        own = gather(terms, inside)
        if step == SWAP_STEP:
            return own, gather(lax.ppermute(own, "col", swaps), inside)
        return (gather(gather(own, across), inside),)

    terms, carried = pl.pallas_call(
        first_kernel,
        in_specs=[HBM] * 7,
        out_specs=[VMEM] * 2,
        out_shape=[slots, field],
        scratch_shapes=[
            pltpu.VMEM(wet.shape, wet.dtype),
            pltpu.VMEM(implicit.shape, implicit.dtype),
            pltpu.VMEM(tiles.shape, tiles.dtype),
            scratch,
            planes,
            rows,
            pltpu.VMEM((1, SLOTS), jnp.int32),
            pltpu.SMEM((1,), jnp.int32),
            pltpu.SemaphoreType.DMA((PARTS + 8,)),
        ],
        compiler_params=pltpu.CompilerParams(vmem_limit_bytes=62 * MIB),
        name="first_step",
    )(tile_rows, tile_cols.reshape(1, SLOTS), tile_count, wet, final_adjoint, implicit, tiles)
    for section in range(STEPS - 2, -1, -1):
        gots = exchange(terms, STEPS - 2 - section)
        terms, carried = pl.pallas_call(
            functools.partial(next_kernel, section, len(gots)),
            in_specs=[VMEM] * len(gots) + [HBM] + [VMEM] * 5,
            out_specs=[VMEM] * 2,
            out_shape=[slots, field],
            scratch_shapes=[scratch, planes, scratch, rows, pltpu.SemaphoreType.DMA],
            compiler_params=pltpu.CompilerParams(vmem_limit_bytes=24 * MIB),
            name="next_step",
        )(*gots, tile_rows, wet, carried, implicit, states, tiles)
    gots = exchange(terms, STEPS - 1)
    return pl.pallas_call(
        last_kernel,
        in_specs=[VMEM] * (len(gots) + 3),
        out_specs=VMEM,
        out_shape=field,
        scratch_shapes=[scratch],
        compiler_params=pltpu.CompilerParams(vmem_limit_bytes=24 * MIB),
        name="last_step",
    )(*gots, wet, carried, states)


def solution(mesh):
    in_specs = (
        P(None, None, "col"),
        P(None, None, None, "col"),
        P(None, None, "col"),
        P("col"),
        P("col"),
        P("col"),
        P("col", None, None),
        P("col"),
    )
    out_specs = P(None, None, "col")
    return jax.shard_map(shards, mesh=mesh, in_specs=in_specs, out_specs=out_specs, check_vma=False)
```

time: 70.5 us -> 59.1 us (0.84)
  the two profiles are of different devices: /device:TPU:1 before, /device:TPU:7 now
where the time goes in v2:
time: 59.1 us; the launch traced here: 58.2 us
  blocking collectives  39.3 us (66%)
  starting transfers between devices  7.59 us (13%)
  Pallas kernels  7.06 us (12%)
  waiting for transfers between devices  3.4 us (6%)
  between operations  0.76 us (1%)
    all_gather x8, blocking collectives, gather(): return lax.all_gather(x, 'col', axis_index_groups=groups, tiled=True)  39.3 us
    ppermute x1, starting transfers between devices, exchange(): return (own, gather(lax.ppermute(own, 'col', swaps), inside))  7.59 us
    ppermute x1, waiting for transfers between devices, exchange(): return (own, gather(lax.ppermute(own, 'col', swaps), inside))  3.4 us
    pallas_call x1, Pallas kernels, shards(): pl.pallas_call(first_kernel, in_specs=[HBM] * 7, out_specs=[VMEM] * 2, ou...  3.12 us
    pallas_call x2, Pallas kernels, shards(): pl.pallas_call(functools.partial(next_kernel, section, len(gots)), in_spe...  2.94 us
  transfers between devices with their start and end apart: 1, of which 1 were waited for; matrix products, arithmetic and copies ran while one was open for 0% of the time, Pallas kernels for 0%

profile of v2, /device:TPU:7, one launch (start us, length us, event | category | flops | bytes accessed | tf_op | source)
XLA Modules:
  0.0 58.2 jit_solution(8826447941507775721)
XLA Ops:
  0.7 0.0 copy-start.1
  0.7 3.1 %first_step.1 = (f32[224,128]{1,0:T(8,128)}, f32[7,50,128]{2,1,0:T(8,128)}) custom-call(s32[30]{0:T(128)} %refs_2_.1, s32[1,30]{1,0:T(1,128)} %bitcast.6, s32[1]{0:T(128)S(6)} %copy.9.count_h, s32[1,128]{1,0:T(1,128)} %bitcast.2, f32[7,50,128]{2,1,0:T(8,128)} %final_h.1, f32[50,50,128]{2,1,0:T(8,128)} %refs_5_.3, bf16[30,128,128]{2,1,0:T(8,128)(2,1)} %refs_7_.1), custom_call_target="tpu_custom_call" | custom-call | tf_op jit(solution)/shard_map/first_step/pallas_call | solution.py:237
  3.8 0.0 copy-start
  3.8 0.0 copy-start.2
  3.8 0.0 copy-start.3
  3.8 0.0 copy-start.4
  3.8 0.0 copy-start.5
  3.9 2.6 %all_gather.24 = f32[448,128]{1,0:T(8,128)S(1)} all-gather(f32[224,128]{1,0:T(8,128)} %get-tuple-element.11), channel_id=1, replica_groups={{0,1},{2,3},{4,5},{6,7},{8,9},{10,11},{12,13},{14,15},{16,17},{18,19},{..., dimensions={0}, use_global_device_ids=true | all-gather | bytes 344064 | tf_op jit(solution)/shard_map/all_gather | solution.py:229
  6.5 16.0 %all_gather.25 = f32[896,128]{1,0:T(8,128)S(1)} all-gather(f32[448,128]{1,0:T(8,128)S(1)} %all_gather.24), channel_id=1, replica_groups={{0,2},{4,6},{8,10},{12,14},{16,18},{20,22},{24,26},{28,30},{32,34},{36,..., dimensions={0}, use_global_device_ids=true | all-gather | bytes 688128 | tf_op jit(solution)/shard_map/all_gather | solution.py:229
  22.5 2.5 %all_gather.26.refs_0_ = f32[1792,128]{1,0:T(8,128)S(1)} all-gather(f32[896,128]{1,0:T(8,128)S(1)} %all_gather.25), channel_id=1, replica_groups={{0,1},{2,3},{4,5},{6,7},{8,9},{10,11},{12,13},{14,15},{16,17},{18,19},{..., dimensions={0}, use_global_device_ids=true | all-gather | bytes 1376256 | tf_op jit(solution)/shard_map/all_gather | solution.py:229
  24.9 0.0 copy-done.1
  24.9 0.0 copy-done
  24.9 0.0 copy-done.2
  24.9 0.0 copy-done.3
  24.9 0.0 copy-done.4
  25.0 0.0 copy-done.5
  25.0 1.5 %next_step.2 = (f32[224,128]{1,0:T(8,128)S(1)}, f32[7,50,128]{2,1,0:T(8,128)S(1)}) custom-call(f32[1792,128]{1,0:T(8,128)S(1)} %all_gather.26.refs_0_, s32[30]{0:T(128)S(1)} %copy-done.5, s32[1,128]{1,0:T(1,128)S(1)} %bitcast.3, f32[7,50,128]{2,1,0:T(8,128)S(1)} %copy-done.3, f32[50,50,128]{2,1,0:T(8,128)S(1)} %copy-done, f32[3,7,50,128]{3,2,1,0:T(8,128)S(1)} %copy-done.2, ...), custom_call_target="tpu_custom_call" | custom-call | tf_op jit(solution)/shard_map/next_step/pallas_call | solution.py:258
  26.5 2.0 %all_gather.27.refs_0_ = f32[448,128]{1,0:T(8,128)S(1)} all-gather(f32[224,128]{1,0:T(8,128)S(1)} %get-tuple-element.13), channel_id=1, replica_groups={{0,1},{2,3},{4,5},{6,7},{8,9},{10,11},{12,13},{14,15},{16,17},{18,19},{..., dimensions={0}, use_global_device_ids=true | all-gather | bytes 344064 | tf_op jit(solution)/shard_map/all_gather | solution.py:229
  28.5 7.6 %collective-permute-start = (f32[448,128]{1,0:T(8,128)S(1)}, f32[448,128]{1,0:T(8,128)S(1)}, u32[]{:S(2)}, u32[]{:S(2)}) collective-permute-start(f32[448,128]{1,0:T(8,128)S(1)} %all_gather.27.refs_0_), channel_id=1, source_target_pairs={{0,2},{2,0},{4,6},{6,4},{8,10},{10,8},{12,14},{14,12},{16,18},{18,... | collective-permute-start | bytes 688136 | tf_op jit(solution)/shard_map/ppermute | solution.py:234
  36.1 3.4 %collective-permute-done = f32[448,128]{1,0:T(8,128)S(1)} collective-permute-done((f32[448,128]{1,0:T(8,128)S(1)}, f32[448,128]{1,0:T(8,128)S(1)}, u32[]{:S(2)}, u32[]{:S(2)}) %collective-permute-start) | collective-permute-done | bytes 229408 | tf_op jit(solution)/shard_map/ppermute | solution.py:234
  39.5 2.1 %all_gather.28.refs_1_ = f32[896,128]{1,0:T(8,128)S(1)} all-gather(f32[448,128]{1,0:T(8,128)S(1)} %collective-permute-done), channel_id=1, replica_groups={{0,1},{2,3},{4,5},{6,7},{8,9},{10,11},{12,13},{14,15},{16,17},{18,19},{..., dimensions={0}, use_global_device_ids=true | all-gather | bytes 688128 | tf_op jit(solution)/shard_map/all_gather | solution.py:229
  41.6 1.4 %next_step.3 = (f32[224,128]{1,0:T(8,128)S(1)}, f32[7,50,128]{2,1,0:T(8,128)S(1)}) custom-call(f32[448,128]{1,0:T(8,128)S(1)} %all_gather.27.refs_0_, f32[896,128]{1,0:T(8,128)S(1)} %all_gather.28.refs_1_, s32[30]{0:T(128)S(1)} %copy-done.5, s32[1,128]{1,0:T(1,128)S(1)} %bitcast.4, f32[7,50,128]{2,1,0:T(8,128)S(1)} %get-tuple-element.14.refs_4_, ...), custom_call_target="tpu_custom_call" | custom-call | tf_op jit(solution)/shard_map/next_step/pallas_call | solution.py:258
  43.0 2.0 %all_gather.29 = f32[448,128]{1,0:T(8,128)S(1)} all-gather(f32[224,128]{1,0:T(8,128)S(1)} %get-tuple-element.15), channel_id=1, replica_groups={{0,1},{2,3},{4,5},{6,7},{8,9},{10,11},{12,13},{14,15},{16,17},{18,19},{..., dimensions={0}, use_global_device_ids=true | all-gather | bytes 344064 | tf_op jit(solution)/shard_map/all_gather | solution.py:229
  45.0 9.8 %all_gather.30 = f32[896,128]{1,0:T(8,128)S(1)} all-gather(f32[448,128]{1,0:T(8,128)S(1)} %all_gather.29), channel_id=1, replica_groups={{0,2},{4,6},{8,10},{12,14},{16,18},{20,22},{24,26},{28,30},{32,34},{36,..., dimensions={0}, use_global_device_ids=true | all-gather | bytes 688128 | tf_op jit(solution)/shard_map/all_gather | solution.py:229
  54.7 2.5 %all_gather.31.refs_0_ = f32[1792,128]{1,0:T(8,128)S(1)} all-gather(f32[896,128]{1,0:T(8,128)S(1)} %all_gather.30), channel_id=1, replica_groups={{0,1},{2,3},{4,5},{6,7},{8,9},{10,11},{12,13},{14,15},{16,17},{18,19},{..., dimensions={0}, use_global_device_ids=true | all-gather | bytes 1376256 | tf_op jit(solution)/shard_map/all_gather | solution.py:229
  57.2 1.0 %last_step.1 = f32[7,50,128]{2,1,0:T(8,128)} custom-call(f32[1792,128]{1,0:T(8,128)S(1)} %all_gather.31.refs_0_, s32[1,128]{1,0:T(1,128)S(1)} %bitcast.5, f32[7,50,128]{2,1,0:T(8,128)S(1)} %get-tuple-element.16.refs_2_, f32[3,7,50,128]{3,2,1,0:T(8,128)S(1)} %copy-done.2), custom_call_target="tpu_custom_call" | custom-call | tf_op jit(solution)/shard_map/last_step/pallas_call | solution.py:268
Async XLA Ops:
  0.7 24.3 %copy-start.1 = (bf16[30,128,128]{2,1,0:T(8,128)(2,1)S(1)}, bf16[30,128,128]{2,1,0:T(8,128)(2,1)}, u32[]{:S(2)}) copy-start(bf16[30,128,128]{2,1,0:T(8,128)(2,1)} %refs_7_.1) | copy-start | bytes 2949124
  3.8 21.1 %copy-start = (f32[50,50,128]{2,1,0:T(8,128)S(1)}, f32[50,50,128]{2,1,0:T(8,128)}, u32[]{:S(2)}) copy-start(f32[50,50,128]{2,1,0:T(8,128)} %refs_5_.3) | copy-start | bytes 3840004
  3.8 21.1 %copy-start.2 = (f32[3,7,50,128]{3,2,1,0:T(8,128)S(1)}, f32[3,7,50,128]{3,2,1,0:T(8,128)}, u32[]{:S(2)}) copy-start(f32[3,7,50,128]{3,2,1,0:T(8,128)} %refs_3_.1) | copy-start | bytes 1612804
  3.8 21.1 %copy-start.3 = (f32[7,50,128]{2,1,0:T(8,128)S(1)}, f32[7,50,128]{2,1,0:T(8,128)}, u32[]{:S(2)}) copy-start(f32[7,50,128]{2,1,0:T(8,128)} %get-tuple-element.12.refs_3_) | copy-start | bytes 537604
  3.8 21.1 %copy-start.4 = (s32[128]{0:T(128)S(1)}, s32[128]{0:T(128)}, u32[]{:S(2)}) copy-start(s32[128]{0:T(128)} %param.11) | copy-start | bytes 1540
  3.8 21.1 %copy-start.5 = (s32[30]{0:T(128)S(1)}, s32[30]{0:T(128)}, u32[]{:S(2)}) copy-start(s32[30]{0:T(128)} %refs_2_.1) | copy-start | bytes 364
  28.5 11.0 %collective-permute-start = (f32[448,128]{1,0:T(8,128)S(1)}, f32[448,128]{1,0:T(8,128)S(1)}, u32[]{:S(2)}, u32[]{:S(2)}) collective-permute-start(f32[448,128]{1,0:T(8,128)S(1)} %all_gather.27.refs_0_), channel_id=1, source_target_pairs={{0,2},{2,0},{4,6},{6,4},{8,10},{10,8},{12,14},{14,12},{16,18},{18,... | collective-permute-start | bytes 688136 | tf_op jit(solution)/shard_map/ppermute | solution.py:234

commit v3 on v2

--- a/solution.py
+++ b/solution.py
@@ -58,7 +58,7 @@
     return (level_ids < wet).astype(jnp.float32)
 
 
-def advance(adj_ref, implicit_ref, wet, carried_ref, planes, arrive=None, parts=1):
+def product(adj_ref, implicit_ref, arrive=None, parts=1):
     def term(k, acc):
         m = implicit_ref[k]
         return tuple(acc[t] + m * adj_ref[t, pl.ds(k, 1), :] for t in range(TRC))
@@ -67,7 +67,12 @@
     for part in range(parts):
         if arrive is not None:
             arrive(part)
-        acc = lax.fori_loop(part * LEV // parts, (part + 1) * LEV // parts, term, acc, unroll=25)
+        acc = lax.fori_loop(part * LEV // parts, (part + 1) * LEV // parts, term, acc, unroll=min(25, LEV // parts))
+    return acc
+
+
+def advance(adj_ref, implicit_ref, wet, carried_ref, planes):
+    acc = product(adj_ref, implicit_ref)
     mask = wet_mask(wet)
     for t in range(TRC):
         carried = acc[t] * mask
@@ -79,42 +84,50 @@
     origin = lax.axis_index("col") * LEV
     for t in range(TRC):
         out_ref[t * SPAN + 24 : (t + 1) * SPAN, :] = jnp.zeros((8, 128), jnp.float32)
-    for p in range(SLOTS):
+
+    def pick(p):
         row = pl.multiple_of(jnp.clip(rows[p] - origin, 0, LEV - 1) * 8, 8)
         picked = planes[pl.ds(row, 8), :]
         hi = picked.astype(jnp.bfloat16)
         lo = (picked - hi.astype(jnp.float32)).astype(jnp.bfloat16)
-        both = jnp.concatenate([hi, lo], axis=0)
-        prod = jnp.dot(both, tiles_ref[p], preferred_element_type=jnp.float32)
-        out_ref[pl.ds(p, TRC, stride=SPAN), :] = prod[:TRC] + prod[8 : 8 + TRC]
-
-
-def first_kernel(rows_h, cols_h, count_h, wet_h, final_h, implicit_h, tiles_h,
-                 out_ref, carried_ref, wet, implicit, tiles, adj, planes, rows, cols, count, sems):
-    used = [0]
-
-    def begin(src, dst):
-        copy = pltpu.make_async_copy(src, dst, sems.at[used[0]])
-        used[0] += 1
+        return [hi, lo]
+
+    for p in range(0, SLOTS, 2):
+        left = jnp.concatenate(pick(p) + pick(p + 1), axis=0)
+        right = jnp.concatenate([tiles_ref[p], tiles_ref[p + 1]], axis=1)
+        prod = jnp.dot(left, right, preferred_element_type=jnp.float32)
+        out_ref[pl.ds(p, TRC, stride=SPAN), :] = prod[:TRC, :128] + prod[8 : 8 + TRC, :128]
+        out_ref[pl.ds(p + 1, TRC, stride=SPAN), :] = prod[16 : 16 + TRC, 128:] + prod[24 : 24 + TRC, 128:]
+
+
+def first_kernel(final_h, implicit_h, out_ref, implicit, adj, sems):
+    span = LEV // PARTS
+    copies = [pltpu.make_async_copy(final_h, adj, sems.at[PARTS])]
+    for i in range(PARTS):
+        part = pl.ds(i * span, span)
+        copies.append(pltpu.make_async_copy(implicit_h.at[part], implicit.at[part], sems.at[i]))
+    for copy in copies:
         copy.start()
-        return copy
-
-    span = LEV // PARTS
-    small = [begin(final_h, adj), begin(wet_h, wet)]
-    parts = [begin(implicit_h.at[pl.ds(i * span, span)], implicit.at[pl.ds(i * span, span)]) for i in range(PARTS)]
-    small += [begin(cols_h, cols), begin(count_h, count), begin(rows_h, rows)]
-    half = SLOTS // 2
-    late = [begin(tiles_h.at[pl.ds(i * half, half)], tiles.at[pl.ds(i * half, half)]) for i in range(2)]
-    for copy in small[:2]:
-        copy.wait()
-    advance(adj, implicit, wet[...], carried_ref, planes, lambda i: parts[i].wait(), PARTS)
-    for copy in small[2:] + late:
-        copy.wait()
-    make_terms(planes, tiles, rows, out_ref)
+    copies[0].wait()
+    acc = product(adj, implicit, lambda i: copies[i + 1].wait(), PARTS)
+    for t in range(TRC):
+        out_ref[t] = acc[t]
+
+
+def first_terms(rows_h, cols, count, wet, product_ref, tiles_ref, out_ref, carried_ref, planes, rows, sem):
+    copy = pltpu.make_async_copy(rows_h, rows, sem)
+    copy.start()
+    mask = wet_mask(wet[...])
+    for t in range(TRC):
+        carried = product_ref[t] * mask
+        planes[pl.ds(t, LEV, stride=8), :] = carried
+        carried_ref[t] = carried
     place = cols[...] - (lax.axis_index("col") - REACH) * LEV
     key = sum((place >= LEV * j).astype(jnp.int32) for j in range(1, KEYS))
     lane = lax.broadcasted_iota(jnp.int32, (1, SLOTS), 1)
-    code = jnp.where(lane < count[0], place + (KEY - LEV) * key, -1).astype(jnp.float32)
+    code = jnp.where(lane < count[...], place + (KEY - LEV) * key, -1).astype(jnp.float32)
+    copy.wait()
+    make_terms(planes, tiles_ref, rows, out_ref)
     out_ref[INFO : INFO + 1, :] = jnp.full((1, 128), -1.0, jnp.float32)
     for i in range(128 // SPAN):
         out_ref[INFO : INFO + 1, i * SPAN : i * SPAN + SLOTS] = code
@@ -207,9 +220,10 @@
 VMEM = pl.BlockSpec(memory_space=pltpu.VMEM)
 HBM = pl.BlockSpec(memory_space=pltpu.HBM)
 f32 = jnp.float32
-PARTS = 2
+PARTS = 5
 SWAP_STEP = 1
 MIB = 1024 * 1024
+FIRST_GRANT = 56255054
 
 
 def shards(final_adjoint, states, implicit, wet_levels, tile_rows, tile_cols, tiles, tile_count):
@@ -234,25 +248,24 @@
             return own, gather(lax.ppermute(own, "col", swaps), inside)
         return (gather(gather(own, across), inside),)
 
+    first = pl.pallas_call(
+        first_kernel,
+        in_specs=[HBM] * 2,
+        out_specs=VMEM,
+        out_shape=field,
+        scratch_shapes=[pltpu.VMEM(implicit.shape, f32), scratch, pltpu.SemaphoreType.DMA((PARTS + 1,))],
+        compiler_params=pltpu.CompilerParams(vmem_limit_bytes=FIRST_GRANT),
+        name="first_step",
+    )(final_adjoint, implicit)
     terms, carried = pl.pallas_call(
-        first_kernel,
-        in_specs=[HBM] * 7,
+        first_terms,
+        in_specs=[HBM] + [VMEM] * 5,
         out_specs=[VMEM] * 2,
         out_shape=[slots, field],
-        scratch_shapes=[
-            pltpu.VMEM(wet.shape, wet.dtype),
-            pltpu.VMEM(implicit.shape, implicit.dtype),
-            pltpu.VMEM(tiles.shape, tiles.dtype),
-            scratch,
-            planes,
-            rows,
-            pltpu.VMEM((1, SLOTS), jnp.int32),
-            pltpu.SMEM((1,), jnp.int32),
-            pltpu.SemaphoreType.DMA((PARTS + 8,)),
-        ],
-        compiler_params=pltpu.CompilerParams(vmem_limit_bytes=62 * MIB),
-        name="first_step",
-    )(tile_rows, tile_cols.reshape(1, SLOTS), tile_count, wet, final_adjoint, implicit, tiles)
+        scratch_shapes=[planes, rows, pltpu.SemaphoreType.DMA],
+        compiler_params=pltpu.CompilerParams(vmem_limit_bytes=24 * MIB),
+        name="first_terms",
+    )(tile_rows, tile_cols.reshape(1, SLOTS), tile_count.reshape(1, 1), wet, first, tiles)
     for section in range(STEPS - 2, -1, -1):
         gots = exchange(terms, STEPS - 2 - section)
         terms, carried = pl.pallas_call(

time: 59.1 us -> 58.2 us (0.985)
  Pallas kernels: 7.06 us -> 6.3 us
    pallas_call x1 -> x2, Pallas kernels: 3.12 us -> 2.61 us  [the longest x1 1.78 us: shards(): pl.pallas_call(first_kernel, in_specs=[HBM] * 2, out_specs=VMEM, out_shap...]
where the time goes in v3:
time: 58.2 us; the launch traced here: 57.3 us
  blocking collectives  39.1 us (67%)
  starting transfers between devices  7.59 us (13%)
  Pallas kernels  6.3 us (11%)
  waiting for transfers between devices  3.4 us (6%)
  between operations  0.83 us (1%)
    all_gather x8, blocking collectives, gather(): return lax.all_gather(x, 'col', axis_index_groups=groups, tiled=True)  39.1 us
    ppermute x1, starting transfers between devices, exchange(): return (own, gather(lax.ppermute(own, 'col', swaps), inside))  7.59 us
    ppermute x1, waiting for transfers between devices, exchange(): return (own, gather(lax.ppermute(own, 'col', swaps), inside))  3.4 us
    pallas_call x2, Pallas kernels, shards(): pl.pallas_call(functools.partial(next_kernel, section, len(gots)), in_spe...  2.69 us
    pallas_call x1, Pallas kernels, shards(): pl.pallas_call(first_kernel, in_specs=[HBM] * 2, out_specs=VMEM, out_shap...  1.78 us
  transfers between devices with their start and end apart: 1, of which 1 were waited for; matrix products, arithmetic and copies ran while one was open for 0% of the time, Pallas kernels for 0%

profile of v3, /device:TPU:7, one launch (start us, length us, event | category | flops | bytes accessed | tf_op | source)
XLA Modules:
  0.0 57.3 jit_solution(12637371330307045865)
XLA Ops:
  0.0 0.0 copy-start.1
  0.0 0.0 copy-start.4
  0.0 0.0 copy-start.5
  0.0 0.0 copy-start.3
  0.7 1.8 %first_step.1.product_ref = f32[7,50,128]{2,1,0:T(8,128)S(1)} custom-call(f32[7,50,128]{2,1,0:T(8,128)} %final_h.1, f32[50,50,128]{2,1,0:T(8,128)} %refs_5_.3), custom_call_target="tpu_custom_call" | custom-call | tf_op jit(solution)/shard_map/first_step/pallas_call | solution.py:251
  2.5 0.0 copy-done.1
  2.5 0.0 copy-done.4
  2.6 0.0 copy-done.5
  2.6 0.0 copy-done.3
  2.6 0.8 %first_terms.1 = (f32[224,128]{1,0:T(8,128)S(1)}, f32[7,50,128]{2,1,0:T(8,128)S(1)}) custom-call(s32[30]{0:T(128)S(1)} %copy-done.4, s32[1,30]{1,0:T(1,128)S(1)} %bitcast.8, s32[1,1]{1,0:T(1,128)} %bitcast.3.count, s32[1,128]{1,0:T(1,128)S(1)} %bitcast.4, f32[7,50,128]{2,1,0:T(8,128)S(1)} %first_step.1.product_ref, bf16[30,128,128]{2,1,0:T(8,128)(2,1)S(1)} %copy-done.1), custom_call_target="tpu_custom_call" | custom-call | tf_op jit(solution)/shard_map/first_terms/pallas_call | solution.py:260
  3.4 0.0 copy-start
  3.4 0.0 copy-start.2
  3.4 2.4 %all_gather.24 = f32[448,128]{1,0:T(8,128)S(1)} all-gather(f32[224,128]{1,0:T(8,128)S(1)} %get-tuple-element.11), channel_id=1, replica_groups={{0,1},{2,3},{4,5},{6,7},{8,9},{10,11},{12,13},{14,15},{16,17},{18,19},{..., dimensions={0}, use_global_device_ids=true | all-gather | bytes 344064 | tf_op jit(solution)/shard_map/all_gather | solution.py:243
  5.9 16.0 %all_gather.25 = f32[896,128]{1,0:T(8,128)S(1)} all-gather(f32[448,128]{1,0:T(8,128)S(1)} %all_gather.24), channel_id=1, replica_groups={{0,2},{4,6},{8,10},{12,14},{16,18},{20,22},{24,26},{28,30},{32,34},{36,..., dimensions={0}, use_global_device_ids=true | all-gather | bytes 688128 | tf_op jit(solution)/shard_map/all_gather | solution.py:243
  21.8 2.5 %all_gather.26.refs_0_ = f32[1792,128]{1,0:T(8,128)S(1)} all-gather(f32[896,128]{1,0:T(8,128)S(1)} %all_gather.25), channel_id=1, replica_groups={{0,1},{2,3},{4,5},{6,7},{8,9},{10,11},{12,13},{14,15},{16,17},{18,19},{..., dimensions={0}, use_global_device_ids=true | all-gather | bytes 1376256 | tf_op jit(solution)/shard_map/all_gather | solution.py:243
  24.3 0.0 copy-done
  24.3 0.0 copy-done.2
  24.3 1.4 %next_step.2 = (f32[224,128]{1,0:T(8,128)S(1)}, f32[7,50,128]{2,1,0:T(8,128)S(1)}) custom-call(f32[1792,128]{1,0:T(8,128)S(1)} %all_gather.26.refs_0_, s32[30]{0:T(128)S(1)} %copy-done.4, s32[1,128]{1,0:T(1,128)S(1)} %bitcast.5, f32[7,50,128]{2,1,0:T(8,128)S(1)} %get-tuple-element.12.refs_3_, f32[50,50,128]{2,1,0:T(8,128)S(1)} %copy-done, ...), custom_call_target="tpu_custom_call" | custom-call | tf_op jit(solution)/shard_map/next_step/pallas_call | solution.py:271
  25.7 2.0 %all_gather.27.refs_0_ = f32[448,128]{1,0:T(8,128)S(1)} all-gather(f32[224,128]{1,0:T(8,128)S(1)} %get-tuple-element.13), channel_id=1, replica_groups={{0,1},{2,3},{4,5},{6,7},{8,9},{10,11},{12,13},{14,15},{16,17},{18,19},{..., dimensions={0}, use_global_device_ids=true | all-gather | bytes 344064 | tf_op jit(solution)/shard_map/all_gather | solution.py:243
  27.7 7.6 %collective-permute-start = (f32[448,128]{1,0:T(8,128)S(1)}, f32[448,128]{1,0:T(8,128)S(1)}, u32[]{:S(2)}, u32[]{:S(2)}) collective-permute-start(f32[448,128]{1,0:T(8,128)S(1)} %all_gather.27.refs_0_), channel_id=1, source_target_pairs={{0,2},{2,0},{4,6},{6,4},{8,10},{10,8},{12,14},{14,12},{16,18},{18,... | collective-permute-start | bytes 688136 | tf_op jit(solution)/shard_map/ppermute | solution.py:248
  35.3 3.4 %collective-permute-done = f32[448,128]{1,0:T(8,128)S(1)} collective-permute-done((f32[448,128]{1,0:T(8,128)S(1)}, f32[448,128]{1,0:T(8,128)S(1)}, u32[]{:S(2)}, u32[]{:S(2)}) %collective-permute-start) | collective-permute-done | bytes 229408 | tf_op jit(solution)/shard_map/ppermute | solution.py:248
  38.7 2.1 %all_gather.28.refs_1_ = f32[896,128]{1,0:T(8,128)S(1)} all-gather(f32[448,128]{1,0:T(8,128)S(1)} %collective-permute-done), channel_id=1, replica_groups={{0,1},{2,3},{4,5},{6,7},{8,9},{10,11},{12,13},{14,15},{16,17},{18,19},{..., dimensions={0}, use_global_device_ids=true | all-gather | bytes 688128 | tf_op jit(solution)/shard_map/all_gather | solution.py:243
  40.8 1.3 %next_step.3 = (f32[224,128]{1,0:T(8,128)S(1)}, f32[7,50,128]{2,1,0:T(8,128)S(1)}) custom-call(f32[448,128]{1,0:T(8,128)S(1)} %all_gather.27.refs_0_, f32[896,128]{1,0:T(8,128)S(1)} %all_gather.28.refs_1_, s32[30]{0:T(128)S(1)} %copy-done.4, s32[1,128]{1,0:T(1,128)S(1)} %bitcast.6, f32[7,50,128]{2,1,0:T(8,128)S(1)} %get-tuple-element.14.refs_4_, ...), custom_call_target="tpu_custom_call" | custom-call | tf_op jit(solution)/shard_map/next_step/pallas_call | solution.py:271
  42.1 2.0 %all_gather.29 = f32[448,128]{1,0:T(8,128)S(1)} all-gather(f32[224,128]{1,0:T(8,128)S(1)} %get-tuple-element.15), channel_id=1, replica_groups={{0,1},{2,3},{4,5},{6,7},{8,9},{10,11},{12,13},{14,15},{16,17},{18,19},{..., dimensions={0}, use_global_device_ids=true | all-gather | bytes 344064 | tf_op jit(solution)/shard_map/all_gather | solution.py:243
  44.1 9.8 %all_gather.30 = f32[896,128]{1,0:T(8,128)S(1)} all-gather(f32[448,128]{1,0:T(8,128)S(1)} %all_gather.29), channel_id=1, replica_groups={{0,2},{4,6},{8,10},{12,14},{16,18},{20,22},{24,26},{28,30},{32,34},{36,..., dimensions={0}, use_global_device_ids=true | all-gather | bytes 688128 | tf_op jit(solution)/shard_map/all_gather | solution.py:243
  53.8 2.5 %all_gather.31.refs_0_ = f32[1792,128]{1,0:T(8,128)S(1)} all-gather(f32[896,128]{1,0:T(8,128)S(1)} %all_gather.30), channel_id=1, replica_groups={{0,1},{2,3},{4,5},{6,7},{8,9},{10,11},{12,13},{14,15},{16,17},{18,19},{..., dimensions={0}, use_global_device_ids=true | all-gather | bytes 1376256 | tf_op jit(solution)/shard_map/all_gather | solution.py:243
  56.3 1.0 %last_step.1 = f32[7,50,128]{2,1,0:T(8,128)} custom-call(f32[1792,128]{1,0:T(8,128)S(1)} %all_gather.31.refs_0_, s32[1,128]{1,0:T(1,128)S(1)} %bitcast.7, f32[7,50,128]{2,1,0:T(8,128)S(1)} %get-tuple-element.16.refs_2_, f32[3,7,50,128]{3,2,1,0:T(8,128)S(1)} %copy-done.2), custom_call_target="tpu_custom_call" | custom-call | tf_op jit(solution)/shard_map/last_step/pallas_call | solution.py:281
Async XLA Ops:
  0.0 2.5 %copy-start.1 = (bf16[30,128,128]{2,1,0:T(8,128)(2,1)S(1)}, bf16[30,128,128]{2,1,0:T(8,128)(2,1)}, u32[]{:S(2)}) copy-start(bf16[30,128,128]{2,1,0:T(8,128)(2,1)} %refs_7_.1) | copy-start | bytes 2949124
  0.0 2.5 %copy-start.4 = (s32[30]{0:T(128)S(1)}, s32[30]{0:T(128)}, u32[]{:S(2)}) copy-start(s32[30]{0:T(128)} %refs_2_.1) | copy-start | bytes 364
  0.0 2.6 %copy-start.5 = (s32[30]{0:T(128)S(1)}, s32[30]{0:T(128)}, u32[]{:S(2)}) copy-start(s32[30]{0:T(128)} %param.13) | copy-start | bytes 364
  0.0 2.6 %copy-start.3 = (s32[128]{0:T(128)S(1)}, s32[128]{0:T(128)}, u32[]{:S(2)}) copy-start(s32[128]{0:T(128)} %param.11) | copy-start | bytes 1540
  3.4 20.9 %copy-start = (f32[50,50,128]{2,1,0:T(8,128)S(1)}, f32[50,50,128]{2,1,0:T(8,128)}, u32[]{:S(2)}) copy-start(f32[50,50,128]{2,1,0:T(8,128)} %refs_5_.3) | copy-start | bytes 3840004
  3.4 20.9 %copy-start.2 = (f32[3,7,50,128]{3,2,1,0:T(8,128)S(1)}, f32[3,7,50,128]{3,2,1,0:T(8,128)}, u32[]{:S(2)}) copy-start(f32[3,7,50,128]{3,2,1,0:T(8,128)} %refs_3_.1) | copy-start | bytes 1612804
  27.7 11.0 %collective-permute-start = (f32[448,128]{1,0:T(8,128)S(1)}, f32[448,128]{1,0:T(8,128)S(1)}, u32[]{:S(2)}, u32[]{:S(2)}) collective-permute-start(f32[448,128]{1,0:T(8,128)S(1)} %all_gather.27.refs_0_), channel_id=1, source_target_pairs={{0,2},{2,0},{4,6},{6,4},{8,10},{10,8},{12,14},{14,12},{16,18},{18,... | collective-permute-start | bytes 688136 | tf_op jit(solution)/shard_map/ppermute | solution.py:248

commit v4 on v3

--- a/solution.py
+++ b/solution.py
@@ -242,11 +242,17 @@
     def gather(x, groups):
         return lax.all_gather(x, "col", axis_index_groups=groups, tiled=True)
 
+    me = lax.axis_index("col")
+    second_of_pair = lax.rem(lax.div(me, 2) + me, 2) == 1
+
     def exchange(terms, step):
         own = gather(terms, inside)
         if step == SWAP_STEP:
-            return own, gather(lax.ppermute(own, "col", swaps), inside)
-        return (gather(gather(own, across), inside),)
+            met = lax.ppermute(own, "col", swaps)
+        else:
+            both = gather(own, across)
+            met = jnp.where(second_of_pair, both[: 2 * CHUNK], both[2 * CHUNK :])
+        return own, gather(met, inside)
 
     first = pl.pallas_call(
         first_kernel,

time: 58.2 us -> 57.5 us (0.988)
  blocking collectives: 39.1 us -> 38.5 us
    all_gather x8, blocking collectives: 39.1 us -> 38.5 us  [gather(): return lax.all_gather(x, 'col', axis_index_groups=groups, tiled=True)]
where the time goes in v4:
time: 57.5 us; the launch traced here: 56.6 us
  blocking collectives  38.5 us (67%)
  starting transfers between devices  7.59 us (13%)
  Pallas kernels  6.14 us (11%)
  waiting for transfers between devices  3.4 us (6%)
  between operations  0.85 us (1%)
    all_gather x8, blocking collectives, gather(): return lax.all_gather(x, 'col', axis_index_groups=groups, tiled=True)  38.5 us
    ppermute x1, starting transfers between devices, exchange(): met = lax.ppermute(own, 'col', swaps)  7.59 us
    ppermute x1, waiting for transfers between devices, exchange(): met = lax.ppermute(own, 'col', swaps)  3.4 us
    pallas_call x2, Pallas kernels, shards(): pl.pallas_call(functools.partial(next_kernel, section, len(gots)), in_spe...  2.59 us
    pallas_call x1, Pallas kernels, shards(): pl.pallas_call(first_kernel, in_specs=[HBM] * 2, out_specs=VMEM, out_shap...  1.78 us
  transfers between devices with their start and end apart: 1, of which 1 were waited for; matrix products, arithmetic and copies ran while one was open for 0% of the time, Pallas kernels for 0%

profile of v4, /device:TPU:7, one launch (start us, length us, event | category | flops | bytes accessed | tf_op | source)
XLA Modules:
  0.0 56.6 jit_solution(15199641186747309077)
XLA Ops:
  0.0 0.0 copy-start.1
  0.0 0.0 copy-start.4
  0.0 0.0 copy-start.5
  0.0 0.0 copy-start.3
  0.8 1.8 %first_step.1.product_ref = f32[7,50,128]{2,1,0:T(8,128)S(1)} custom-call(f32[7,50,128]{2,1,0:T(8,128)} %final_h.1, f32[50,50,128]{2,1,0:T(8,128)} %refs_5_.3), custom_call_target="tpu_custom_call" | custom-call | tf_op jit(solution)/shard_map/first_step/pallas_call | solution.py:257
  2.5 0.0 copy-done.1
  2.6 0.0 copy-done.4
  2.6 0.0 copy-done.5
  2.6 0.0 copy-done.3
  2.6 0.8 %first_terms.1 = (f32[224,128]{1,0:T(8,128)S(1)}, f32[7,50,128]{2,1,0:T(8,128)S(1)}) custom-call(s32[30]{0:T(128)S(1)} %copy-done.4, s32[1,30]{1,0:T(1,128)S(1)} %bitcast.8, s32[1,1]{1,0:T(1,128)} %bitcast.3.count, s32[1,128]{1,0:T(1,128)S(1)} %bitcast.4, f32[7,50,128]{2,1,0:T(8,128)S(1)} %first_step.1.product_ref, bf16[30,128,128]{2,1,0:T(8,128)(2,1)S(1)} %copy-done.1), custom_call_target="tpu_custom_call" | custom-call | tf_op jit(solution)/shard_map/first_terms/pallas_call | solution.py:266
  3.4 0.0 copy-start
  3.4 0.0 copy-start.2
  3.4 2.4 %all_gather.24.refs_0_ = f32[448,128]{1,0:T(8,128)S(1)} all-gather(f32[224,128]{1,0:T(8,128)S(1)} %get-tuple-element.11), channel_id=1, replica_groups={{0,1},{2,3},{4,5},{6,7},{8,9},{10,11},{12,13},{14,15},{16,17},{18,19},{..., dimensions={0}, use_global_device_ids=true | all-gather | bytes 344064 | tf_op jit(solution)/shard_map/all_gather | solution.py:243
  5.9 16.0 %all_gather.25 = f32[896,128]{1,0:T(8,128)S(1)} all-gather(f32[448,128]{1,0:T(8,128)S(1)} %all_gather.24.refs_0_), channel_id=1, replica_groups={{0,2},{4,6},{8,10},{12,14},{16,18},{20,22},{24,26},{28,30},{32,34},{36,..., dimensions={0}, use_global_device_ids=true | all-gather | bytes 688128 | tf_op jit(solution)/shard_map/all_gather | solution.py:243
  21.9 2.1 %all_gather.26.refs_1_ = f32[896,128]{1,0:T(8,128)S(1)} all-gather(f32[448,128]{1,0:T(8,128)S(1)} %slice_select_fusion.1), channel_id=1, replica_groups={{0,1},{2,3},{4,5},{6,7},{8,9},{10,11},{12,13},{14,15},{16,17},{18,19},{..., dimensions={0}, use_global_device_ids=true | all-gather | bytes 688128 | tf_op jit(solution)/shard_map/all_gather | solution.py:243
  24.0 0.0 copy-done
  24.0 0.0 copy-done.2
  24.0 1.3 %next_step.2 = (f32[224,128]{1,0:T(8,128)S(1)}, f32[7,50,128]{2,1,0:T(8,128)S(1)}) custom-call(f32[448,128]{1,0:T(8,128)S(1)} %all_gather.24.refs_0_, f32[896,128]{1,0:T(8,128)S(1)} %all_gather.26.refs_1_, s32[30]{0:T(128)S(1)} %copy-done.4, s32[1,128]{1,0:T(1,128)S(1)} %bitcast.5, f32[7,50,128]{2,1,0:T(8,128)S(1)} %get-tuple-element.12.refs_4_, ...), custom_call_target="tpu_custom_call" | custom-call | tf_op jit(solution)/shard_map/next_step/pallas_call | solution.py:277
  25.3 2.0 %all_gather.27.refs_0_ = f32[448,128]{1,0:T(8,128)S(1)} all-gather(f32[224,128]{1,0:T(8,128)S(1)} %get-tuple-element.13), channel_id=1, replica_groups={{0,1},{2,3},{4,5},{6,7},{8,9},{10,11},{12,13},{14,15},{16,17},{18,19},{..., dimensions={0}, use_global_device_ids=true | all-gather | bytes 344064 | tf_op jit(solution)/shard_map/all_gather | solution.py:243
  27.3 7.6 %collective-permute-start = (f32[448,128]{1,0:T(8,128)S(1)}, f32[448,128]{1,0:T(8,128)S(1)}, u32[]{:S(2)}, u32[]{:S(2)}) collective-permute-start(f32[448,128]{1,0:T(8,128)S(1)} %all_gather.27.refs_0_), channel_id=1, source_target_pairs={{0,2},{2,0},{4,6},{6,4},{8,10},{10,8},{12,14},{14,12},{16,18},{18,... | collective-permute-start | bytes 688136 | tf_op jit(solution)/shard_map/ppermute | solution.py:251
  34.9 3.4 %collective-permute-done = f32[448,128]{1,0:T(8,128)S(1)} collective-permute-done((f32[448,128]{1,0:T(8,128)S(1)}, f32[448,128]{1,0:T(8,128)S(1)}, u32[]{:S(2)}, u32[]{:S(2)}) %collective-permute-start) | collective-permute-done | bytes 229408 | tf_op jit(solution)/shard_map/ppermute | solution.py:251
  38.3 2.1 %all_gather.28.refs_1_ = f32[896,128]{1,0:T(8,128)S(1)} all-gather(f32[448,128]{1,0:T(8,128)S(1)} %collective-permute-done), channel_id=1, replica_groups={{0,1},{2,3},{4,5},{6,7},{8,9},{10,11},{12,13},{14,15},{16,17},{18,19},{..., dimensions={0}, use_global_device_ids=true | all-gather | bytes 688128 | tf_op jit(solution)/shard_map/all_gather | solution.py:243
  40.4 1.3 %next_step.3 = (f32[224,128]{1,0:T(8,128)S(1)}, f32[7,50,128]{2,1,0:T(8,128)S(1)}) custom-call(f32[448,128]{1,0:T(8,128)S(1)} %all_gather.27.refs_0_, f32[896,128]{1,0:T(8,128)S(1)} %all_gather.28.refs_1_, s32[30]{0:T(128)S(1)} %copy-done.4, s32[1,128]{1,0:T(1,128)S(1)} %bitcast.6, f32[7,50,128]{2,1,0:T(8,128)S(1)} %get-tuple-element.14.refs_4_, ...), custom_call_target="tpu_custom_call" | custom-call | tf_op jit(solution)/shard_map/next_step/pallas_call | solution.py:277
  41.7 2.0 %all_gather.29.refs_0_ = f32[448,128]{1,0:T(8,128)S(1)} all-gather(f32[224,128]{1,0:T(8,128)S(1)} %get-tuple-element.15), channel_id=1, replica_groups={{0,1},{2,3},{4,5},{6,7},{8,9},{10,11},{12,13},{14,15},{16,17},{18,19},{..., dimensions={0}, use_global_device_ids=true | all-gather | bytes 344064 | tf_op jit(solution)/shard_map/all_gather | solution.py:243
  43.7 9.8 %all_gather.30 = f32[896,128]{1,0:T(8,128)S(1)} all-gather(f32[448,128]{1,0:T(8,128)S(1)} %all_gather.29.refs_0_), channel_id=1, replica_groups={{0,2},{4,6},{8,10},{12,14},{16,18},{20,22},{24,26},{28,30},{32,34},{36,..., dimensions={0}, use_global_device_ids=true | all-gather | bytes 688128 | tf_op jit(solution)/shard_map/all_gather | solution.py:243
  53.5 2.1 %all_gather.31.refs_1_ = f32[896,128]{1,0:T(8,128)S(1)} all-gather(f32[448,128]{1,0:T(8,128)S(1)} %slice_select_fusion), channel_id=1, replica_groups={{0,1},{2,3},{4,5},{6,7},{8,9},{10,11},{12,13},{14,15},{16,17},{18,19},{..., dimensions={0}, use_global_device_ids=true | all-gather | bytes 688128 | tf_op jit(solution)/shard_map/all_gather | solution.py:243
  55.6 0.9 %last_step.1 = f32[7,50,128]{2,1,0:T(8,128)} custom-call(f32[448,128]{1,0:T(8,128)S(1)} %all_gather.29.refs_0_, f32[896,128]{1,0:T(8,128)S(1)} %all_gather.31.refs_1_, s32[1,128]{1,0:T(1,128)S(1)} %bitcast.7, f32[7,50,128]{2,1,0:T(8,128)S(1)} %get-tuple-element.16.refs_3_, f32[3,7,50,128]{3,2,1,0:T(8,128)S(1)} %copy-done.2), custom_call_target="tpu_custom_call" | custom-call | tf_op jit(solution)/shard_map/last_step/pallas_call | solution.py:287
  (2 shorter events, 0.1 us)
Async XLA Ops:
  0.0 2.5 %copy-start.1 = (bf16[30,128,128]{2,1,0:T(8,128)(2,1)S(1)}, bf16[30,128,128]{2,1,0:T(8,128)(2,1)}, u32[]{:S(2)}) copy-start(bf16[30,128,128]{2,1,0:T(8,128)(2,1)} %refs_7_.3) | copy-start | bytes 2949124
  0.0 2.6 %copy-start.4 = (s32[30]{0:T(128)S(1)}, s32[30]{0:T(128)}, u32[]{:S(2)}) copy-start(s32[30]{0:T(128)} %refs_2_.3) | copy-start | bytes 364
  0.0 2.6 %copy-start.5 = (s32[30]{0:T(128)S(1)}, s32[30]{0:T(128)}, u32[]{:S(2)}) copy-start(s32[30]{0:T(128)} %param.13) | copy-start | bytes 364
  0.0 2.6 %copy-start.3 = (s32[128]{0:T(128)S(1)}, s32[128]{0:T(128)}, u32[]{:S(2)}) copy-start(s32[128]{0:T(128)} %param.11) | copy-start | bytes 1540
  3.4 20.6 %copy-start = (f32[50,50,128]{2,1,0:T(8,128)S(1)}, f32[50,50,128]{2,1,0:T(8,128)}, u32[]{:S(2)}) copy-start(f32[50,50,128]{2,1,0:T(8,128)} %refs_5_.3) | copy-start | bytes 3840004
  3.4 20.6 %copy-start.2 = (f32[3,7,50,128]{3,2,1,0:T(8,128)S(1)}, f32[3,7,50,128]{3,2,1,0:T(8,128)}, u32[]{:S(2)}) copy-start(f32[3,7,50,128]{3,2,1,0:T(8,128)} %refs_4_.1) | copy-start | bytes 1612804
  27.3 11.0 %collective-permute-start = (f32[448,128]{1,0:T(8,128)S(1)}, f32[448,128]{1,0:T(8,128)S(1)}, u32[]{:S(2)}, u32[]{:S(2)}) collective-permute-start(f32[448,128]{1,0:T(8,128)S(1)} %all_gather.27.refs_0_), channel_id=1, source_target_pairs={{0,2},{2,0},{4,6},{6,4},{8,10},{10,8},{12,14},{14,12},{16,18},{18,... | collective-permute-start | bytes 688136 | tf_op jit(solution)/shard_map/ppermute | solution.py:251

commit v5 on v4

v5 whole, which is shorter than its diff:
```python
import functools
import jax
import jax.numpy as jnp
from jax import lax
from jax.experimental import pallas as pl
from jax.experimental.pallas import tpu as pltpu
from jax.sharding import PartitionSpec as P

STEPS = 3
TRC = 7
LEV = 50
PAD = 56
SLOTS = 30
REACH = 2
KEYS = 2 * REACH + 1
time_step = 0.5
SPAN = 32
INFO = SLOTS
CHUNK = TRC * SPAN
KEY = 64
NONE = -1000.0


def pull_back(states, carried, light):
    phosphate, _, oxygen, plankton, grazers, detritus, nitrate = states
    c_pho, c_dis, c_oxy, c_pla, c_gra, c_det, c_nit = carried
    rp = 1.0 / (0.03 + phosphate)
    rn = 1.0 / (0.5 + nitrate)
    ro = 1.0 / (1.0 + oxygen)
    p2 = plankton * plankton
    rg = 1.0 / (0.1 + p2)
    mix = c_pho - 1.2 * c_oxy + 1.6 * c_nit
    a_growth = 0.1 * c_dis + c_pla - mix
    a_grazing = 0.3 * c_pho - c_pla + 0.7 * c_gra
    a_mortality = 0.1 * c_dis - c_pla + 0.9 * c_det
    a_remineral = mix - c_det
    a_decay = mix - c_dis
    a_loss = c_det - c_gra
    fp = phosphate * rp
    fn = nitrate * rn
    lg = (1.2 * light) * a_growth
    lgp = lg * plankton
    d_pho = lgp * fn * (0.03 * rp * rp)
    d_nit = lgp * fp * (0.5 * rn * rn)
    hol = p2 * rg
    ag = 1.9 * a_grazing
    d_pla = lg * fp * fn + ag * grazers * (0.2 * plankton * rg * rg) + 0.06 * plankton * a_mortality
    d_gra = ag * hol + 0.1 * grazers * a_loss
    ar = 0.05 * a_remineral
    d_det = ar * oxygen * ro
    d_oxy = ar * detritus * (ro * ro)
    d_dis = 0.17 * a_decay
    return [d_pho, d_dis, d_oxy, d_pla, d_gra, d_det, d_nit]


def wet_mask(wet):
    level_ids = lax.broadcasted_iota(jnp.int32, (LEV, 128), 0)
    return (level_ids < wet).astype(jnp.float32)


def product(adj_ref, implicit_ref, arrive=None, parts=1, lower=None):
    def term(k, acc):
        m = implicit_ref[k]
        return tuple(acc[t] + m * adj_ref[t, pl.ds(k, 1), :] for t in range(TRC))

    def lower_term(k, acc):
        m = lower[k]
        return tuple(acc[t] + m * adj_ref[t, pl.ds(k + LEV // 2, 1), :] for t in range(TRC))

    acc = tuple(jnp.zeros((LEV, 128), jnp.float32) for _ in range(TRC))
    if lower is not None:
        acc = lax.fori_loop(0, LEV // 2, term, acc, unroll=LEV // 2)
        return lax.fori_loop(0, LEV // 2, lower_term, acc, unroll=LEV // 2)
    for part in range(parts):
        if arrive is not None:
            arrive(part)
        acc = lax.fori_loop(part * LEV // parts, (part + 1) * LEV // parts, term, acc, unroll=min(25, LEV // parts))
    return acc


def carry(acc, wet, states_ref, base_ref, planes, arrive):
    mask = wet_mask(wet)
    level_ids = lax.broadcasted_iota(jnp.int32, (LEV, 128), 0)
    light = jnp.exp(-0.2 * level_ids.astype(jnp.float32))
    carried = [acc[t] * mask for t in range(TRC)]
    for t in range(TRC):
        planes[pl.ds(t, LEV, stride=8), :] = carried[t]
    arrive()
    bio = pull_back([states_ref[t] for t in range(TRC)], carried, light)
    for t in range(TRC):
        base_ref[t] = carried[t] + time_step * bio[t]


def make_terms(planes, tiles_ref, rows, sums, out_ref):
    origin = lax.axis_index("col") * LEV
    for t in range(TRC):
        sums[t * SPAN + 24 : (t + 1) * SPAN, :] = jnp.zeros((8, 128), jnp.float32)

    def pick(p):
        row = pl.multiple_of(jnp.clip(rows[p] - origin, 0, LEV - 1) * 8, 8)
        picked = planes[pl.ds(row, 8), :]
        hi = picked.astype(jnp.bfloat16)
        lo = (picked - hi.astype(jnp.float32)).astype(jnp.bfloat16)
        return [hi, lo]

    for p in range(0, SLOTS, 2):
        left = jnp.concatenate(pick(p) + pick(p + 1), axis=0)
        right = jnp.concatenate([tiles_ref[p], tiles_ref[p + 1]], axis=1)
        prod = jnp.dot(left, right, preferred_element_type=jnp.float32)
        sums[pl.ds(p, 8, stride=SPAN), :] = prod[:8, :128] + prod[8:16, :128]
        sums[pl.ds(p + 1, 8, stride=SPAN), :] = prod[16:24, 128:] + prod[24:, 128:]
    out_ref[...] = sums[:CHUNK, :]


def fetch(implicit_h, implicit, sems):
    span = LEV // PARTS
    copies = []
    for i in range(PARTS):
        part = pl.ds(i * span, span)
        copies.append(pltpu.make_async_copy(implicit_h.at[part], implicit.at[part], sems.at[i]))
        copies[-1].start()
    return lambda i: copies[i].wait()


def first_kernel(final_h, implicit_h, out_ref, implicit, adj, sems):
    copy = pltpu.make_async_copy(final_h, adj, sems.at[PARTS])
    copy.start()
    arrive = fetch(implicit_h, implicit, sems)
    copy.wait()
    acc = product(adj, implicit, arrive, PARTS)
    for t in range(TRC):
        out_ref[t] = acc[t]


def first_terms(rows_h, cols, count, wet, product_ref, states_h, implicit_h, tiles_ref,
                out_ref, base_ref, upper, lower, planes, rows, states, sums, sems):
    halves = []
    for i, half in enumerate((upper, lower)):
        part = implicit_h.at[pl.ds(i * (LEV // 2), LEV // 2)]
        halves.append(pltpu.make_async_copy(part, half, sems.at[2 + i]))
    copy = pltpu.make_async_copy(rows_h, rows, sems.at[0])
    copy.start()
    for half in halves:
        half.start()
    state_copy = pltpu.make_async_copy(states_h.at[STEPS - 1], states, sems.at[1])
    state_copy.start()
    carry([product_ref[t] for t in range(TRC)], wet[...], states, base_ref, planes, state_copy.wait)
    place = cols[...] - (lax.axis_index("col") - REACH) * LEV
    key = sum((place >= LEV * j).astype(jnp.int32) for j in range(1, KEYS))
    lane = lax.broadcasted_iota(jnp.int32, (1, SLOTS), 1)
    code = jnp.where(lane < count[...], place + (KEY - LEV) * key, -1).astype(jnp.float32)
    copy.wait()
    make_terms(planes, tiles_ref, rows, sums, out_ref)
    out_ref[INFO : INFO + 1, :] = jnp.full((1, 128), -1.0, jnp.float32)
    for i in range(128 // SPAN):
        out_ref[INFO : INFO + 1, i * SPAN : i * SPAN + SLOTS] = code
    for half in halves:
        half.wait()


def origins():
    chip = lax.div(lax.axis_index("col"), 2)
    odd = lax.rem(chip, 2)
    return [2 * c + k for c in (chip, chip + 1 - 2 * odd, chip - 1 + 2 * odd) for k in range(2)]


def receive(chunks, take):
    me = lax.axis_index("col")
    lane = lax.broadcasted_iota(jnp.int32, (1, 128), 1)
    level = lax.broadcasted_iota(jnp.int32, (64, 128), 0).astype(jnp.float32)
    bases = [(me - src + REACH) * KEY for src in origins()]
    per = 128 // SPAN
    marks = []
    for first in range(0, len(chunks), per):
        number = min(per, len(chunks) - first)
        codes = jnp.full((1, 128), NONE, jnp.float32)
        for i in range(number):
            here = (lane >= i * SPAN) & (lane < (i + 1) * SPAN)
            ref, at = chunks[first + i]
            found = ref[at + INFO : at + INFO + 1, :] - bases[first + i].astype(jnp.float32)
            codes = jnp.where(here, found, codes)
        marks.append((level == codes).astype(jnp.float32).astype(jnp.bfloat16)[:, : number * SPAN])
    marks = jnp.concatenate(marks, axis=1)
    for t in range(TRC):
        data = jnp.concatenate([ref[at + t * SPAN : at + (t + 1) * SPAN, :] for ref, at in chunks], axis=0)
        hi = data.astype(jnp.bfloat16)
        lo = (data - hi.astype(jnp.float32)).astype(jnp.bfloat16)
        both = jnp.dot(marks, jnp.concatenate([hi, lo], axis=1), preferred_element_type=jnp.float32)
        take(t, both[:LEV, :128] + both[:LEV, 128:])


def chunks_of(gots):
    return [(ref, at) for ref in gots for at in range(0, ref.shape[0], CHUNK)]


def adjoint_into(out_ref, gots, wet_ref, base):
    mask = wet_mask(wet_ref[...])

    def take(t, transport):
        out_ref[t] = mask * (base[t] + transport)

    receive(chunks_of(gots), take)


def next_kernel(section, own_ref, got_ref, rows_h, wet_ref, base_in, upper, lower, states_h, tiles_h,
                out_ref, base_ref, planes, adj, rows, states, tiles_ref, sums, sems):
    tile_copy = pltpu.make_async_copy(tiles_h, tiles_ref, sems.at[0])
    tile_copy.start()
    copy = pltpu.make_async_copy(rows_h, rows, sems.at[1])
    copy.start()
    state_copy = pltpu.make_async_copy(states_h.at[section], states, sems.at[2])
    state_copy.start()
    adjoint_into(adj, (own_ref, got_ref), wet_ref, base_in)
    carry(product(adj, upper, lower=lower), wet_ref[...], states, base_ref, planes, state_copy.wait)
    copy.wait()
    tile_copy.wait()
    make_terms(planes, tiles_ref, rows, sums, out_ref)
    core = lax.rem(lax.axis_index("col"), 2)
    out_ref[INFO : INFO + 1, :] = own_ref[pl.ds(core * CHUNK + INFO, 1), :]


def last_kernel(own_ref, got_ref, wet_ref, base_in, out_ref):
    adjoint_into(out_ref, (own_ref, got_ref), wet_ref, base_in)


VMEM = pl.BlockSpec(memory_space=pltpu.VMEM)
HBM = pl.BlockSpec(memory_space=pltpu.HBM)
f32 = jnp.float32
PARTS = 5
MIB = 1024 * 1024
FIRST_GRANT = 56255054
TERMS_GRANT = 50 * MIB
NEXT_GRANT = int(50.2 * MIB)


def shards(final_adjoint, states, implicit, wet_levels, tile_rows, tile_cols, tiles, tile_count):
    devices = lax.axis_size("col")
    inside = [[2 * c, 2 * c + 1] for c in range(devices // 2)]
    across = [[2 * c, 2 * c + 2] for c in range(0, devices // 2, 2)]
    across += [[2 * c + 1, (2 * c + 3) % devices] for c in range(1, devices // 2, 2)]
    slots = jax.ShapeDtypeStruct((CHUNK, 128), f32)
    field = jax.ShapeDtypeStruct((TRC, LEV, 128), f32)
    scratch = pltpu.VMEM((TRC, LEV, 128), f32)
    planes = pltpu.VMEM((PAD * 8, 128), f32)
    sums = pltpu.VMEM((8 * SPAN, 128), f32)
    matrix = pltpu.VMEM(implicit.shape, f32)
    rows = pltpu.SMEM((SLOTS,), jnp.int32)
    wet = wet_levels.reshape(1, 128)

    def gather(x, groups):
        return lax.all_gather(x, "col", axis_index_groups=groups, tiled=True)

    me = lax.axis_index("col")
    second_of_pair = lax.rem(lax.div(me, 2) + me, 2) == 1

    alone = (me == across[-1][0]) | (me == across[-1][1])

    def exchange(terms):
        own = gather(terms, inside)

        def meet(x):
            both = gather(x, across)
            return jnp.where(second_of_pair, both[: 2 * CHUNK], both[2 * CHUNK :])

        met = lax.cond(alone, jnp.zeros_like, meet, own)
        return own, gather(met, inside)

    first = pl.pallas_call(
        first_kernel,
        in_specs=[HBM] * 2,
        out_specs=VMEM,
        out_shape=field,
        scratch_shapes=[matrix, scratch, pltpu.SemaphoreType.DMA((PARTS + 1,))],
        compiler_params=pltpu.CompilerParams(vmem_limit_bytes=FIRST_GRANT),
        name="first_step",
    )(final_adjoint, implicit)
    half = jax.ShapeDtypeStruct((LEV // 2, LEV, 128), f32)
    terms, base, upper, lower = pl.pallas_call(
        first_terms,
        in_specs=[HBM] + [VMEM] * 4 + [HBM, HBM, VMEM],
        out_specs=[VMEM] * 4,
        out_shape=[slots, field, half, half],
        scratch_shapes=[planes, rows, scratch, sums, pltpu.SemaphoreType.DMA((4,))],
        compiler_params=pltpu.CompilerParams(vmem_limit_bytes=TERMS_GRANT),
        name="first_terms",
    )(tile_rows, tile_cols.reshape(1, SLOTS), tile_count.reshape(1, 1), wet, first, states, implicit, tiles)
    for section in range(STEPS - 2, -1, -1):
        own, got = exchange(terms)
        terms, base = pl.pallas_call(
            functools.partial(next_kernel, section),
            in_specs=[VMEM] * 2 + [HBM] + [VMEM] * 4 + [HBM, HBM],
            out_specs=[VMEM] * 2,
            out_shape=[slots, field],
            scratch_shapes=[
                planes,
                scratch,
                rows,
                scratch,
                pltpu.VMEM(tiles.shape, tiles.dtype),
                sums,
                pltpu.SemaphoreType.DMA((3,)),
            ],
            compiler_params=pltpu.CompilerParams(vmem_limit_bytes=NEXT_GRANT),
            name="next_step",
        )(own, got, tile_rows, wet, base, upper, lower, states, tiles)
    own, got = exchange(terms)
    return pl.pallas_call(
        last_kernel,
        in_specs=[VMEM] * 4,
        out_specs=VMEM,
        out_shape=field,
        compiler_params=pltpu.CompilerParams(vmem_limit_bytes=24 * MIB),
        name="last_step",
    )(own, got, wet, base)


def solution(mesh):
    in_specs = (
        P(None, None, "col"),
        P(None, None, None, "col"),
        P(None, None, "col"),
        P("col"),
        P("col"),
        P("col"),
        P("col", None, None),
        P("col"),
    )
    out_specs = P(None, None, "col")
    return jax.shard_map(shards, mesh=mesh, in_specs=in_specs, out_specs=out_specs, check_vma=False)
```

time: 57.5 us -> 56.5 us (0.983); the launches traced: 56.6 us -> 56.2 us
  blocking collectives: 38.5 us -> 48.1 us
  starting transfers between devices: 7.59 us -> 0 us
  waiting for transfers between devices: 3.4 us -> 0 us
  Pallas kernels: 6.14 us -> 7.02 us
    all_gather x8 -> x9, blocking collectives: 38.5 us -> 48.1 us  [gather(): return lax.all_gather(x, 'col', axis_index_groups=groups, tiled=True)]
    ppermute x1 -> x0, starting transfers between devices: 7.59 us -> none  [exchange(): met = lax.ppermute(own, 'col', swaps)]
    ppermute x1 -> x0, waiting for transfers between devices: 3.4 us -> none  [exchange(): met = lax.ppermute(own, 'col', swaps)]
    pallas_call x4, Pallas kernels: 4.37 us -> 5.24 us  [the longest x2 3 us: shards(): pl.pallas_call(functools.partial(next_kernel, section), in_specs=[VMEM] *...]
  transfers between devices with their start and end apart: 1 -> 0, of which waited for: 1 -> 0; matrix products, arithmetic and copies ran while one was open for 0% -> 0% of each run, Pallas kernels for 0% -> 0%
where the time goes in v5:
time: 56.5 us; the launch traced here: 56.2 us
  blocking collectives  48.1 us (85%)
  Pallas kernels  7.02 us (12%)
  between operations  0.9 us (2%)
    all_gather x9, blocking collectives, gather(): return lax.all_gather(x, 'col', axis_index_groups=groups, tiled=True)  48.1 us
    pallas_call x2, Pallas kernels, shards(): pl.pallas_call(functools.partial(next_kernel, section), in_specs=[VMEM] *...  3 us
    pallas_call x1, Pallas kernels, shards(): pl.pallas_call(first_kernel, in_specs=[HBM] * 2, out_specs=VMEM, out_shap...  1.78 us
    pallas_call x1, Pallas kernels, shards(): pl.pallas_call(first_terms, in_specs=[HBM] + [VMEM] * 4 + [HBM, HBM, VMEM...  1.32 us

profile of v5, /device:TPU:7, one launch (start us, length us, event | category | flops | bytes accessed | tf_op | source)
XLA Modules:
  0.0 56.2 jit_solution(10055975649020393453)
XLA Ops:
  0.0 0.0 copy-start
  0.0 0.0 copy-start.3
  0.0 0.0 copy-start.1
  0.0 0.0 copy-start.4
  0.0 0.0 copy-start.2
  0.8 1.8 %first_step.1.product_ref = f32[7,50,128]{2,1,0:T(8,128)S(1)} custom-call(f32[7,50,128]{2,1,0:T(8,128)} %final_h.1, f32[50,50,128]{2,1,0:T(8,128)} %implicit_h.3), custom_call_target="tpu_custom_call" | custom-call | tf_op jit(solution)/shard_map/first_step/pallas_call | solution.py:268
  2.6 0.0 copy-done
  2.6 0.0 copy-done.3
  2.6 0.0 copy-done.1
  2.6 0.0 copy-done.4
  2.6 0.0 copy-done.2
  2.6 1.3 %first_terms.1 = (f32[224,128]{1,0:T(8,128)S(1)}, f32[7,50,128]{2,1,0:T(8,128)S(1)}, f32[25,50,128]{2,1,0:T(8,128)S(1)}, f32[25,50,128]{2,1,0:T(8,128)S(1)}) custom-call(s32[30]{0:T(128)S(1)} %copy-done.3, s32[1,30]{1,0:T(1,128)S(1)} %bitcast.8, s32[1,1]{1,0:T(1,128)} %bitcast.3.count, s32[1,128]{1,0:T(1,128)S(1)} %bitcast.4, ...), custom_call_target="tpu_custom_call" | custom-call | tf_op jit(solution)/shard_map/first_terms/pallas_call | solution.py:278
  4.0 2.3 %all_gather.27.own_ref = f32[448,128]{1,0:T(8,128)S(1)} all-gather(f32[224,128]{1,0:T(8,128)S(1)} %get-tuple-element.40), channel_id=1, replica_groups={{0,1},{2,3},{4,5},{6,7},{8,9},{10,11},{12,13},{14,15},{16,17},{18,19},{..., dimensions={0}, use_global_device_ids=true | all-gather | bytes 344064 | tf_op jit(solution)/shard_map/all_gather | solution.py:251
  6.3 16.0 %conditional.3 = (f32[448,128]{1,0:T(8,128)S(1)}) conditional(s32[]{:T(128)} %convert_element_type.2, (pred[]{:T(512)}, f32[448,128]{1,0:T(8,128)S(1)}) %tuple.23, () %tuple.24), branch_computations={%region_0.1_spmd, %region_1.2_spmd} | conditional | flops 57344 | bytes 1376265 | solution.py:265
  6.3 16.0 %all_gather.18 = f32[896,128]{1,0:T(8,128)S(1)} all-gather(f32[448,128]{1,0:T(8,128)S(1)} %get-tuple-element.26), channel_id=1, replica_groups={{0,2},{4,6},{8,10},{12,14},{16,18},{20,22},{24,26},{28,30},{32,34},{36,..., dimensions={0}, use_global_device_ids=true | all-gather | bytes 688128 | tf_op jit(solution)/shard_map/cond/branch_0_fun/all_gather | solution.py:251
  22.3 2.1 %all_gather.28.got_ref = f32[896,128]{1,0:T(8,128)S(1)} all-gather(f32[448,128]{1,0:T(8,128)S(1)} %get-tuple-element.48), channel_id=1, replica_groups={{0,1},{2,3},{4,5},{6,7},{8,9},{10,11},{12,13},{14,15},{16,17},{18,19},{..., dimensions={0}, use_global_device_ids=true | all-gather | bytes 688128 | tf_op jit(solution)/shard_map/all_gather | solution.py:251
  24.4 1.5 %next_step.2 = (f32[224,128]{1,0:T(8,128)S(1)}, f32[7,50,128]{2,1,0:T(8,128)S(1)}) custom-call(f32[448,128]{1,0:T(8,128)S(1)} %all_gather.27.own_ref, f32[896,128]{1,0:T(8,128)S(1)} %all_gather.28.got_ref, s32[30]{0:T(128)S(1)} %copy-done.3, s32[1,128]{1,0:T(1,128)S(1)} %bitcast.5, f32[7,50,128]{2,1,0:T(8,128)S(1)} %get-tuple-element.41.base_in, ...), custom_call_target="tpu_custom_call" | custom-call | tf_op jit(solution)/shard_map/next_step/pallas_call | solution.py:289
  25.9 2.0 %all_gather.29.own_ref = f32[448,128]{1,0:T(8,128)S(1)} all-gather(f32[224,128]{1,0:T(8,128)S(1)} %get-tuple-element.44), channel_id=1, replica_groups={{0,1},{2,3},{4,5},{6,7},{8,9},{10,11},{12,13},{14,15},{16,17},{18,19},{..., dimensions={0}, use_global_device_ids=true | all-gather | bytes 344064 | tf_op jit(solution)/shard_map/all_gather | solution.py:251
  27.9 9.8 %conditional.4 = (f32[448,128]{1,0:T(8,128)S(1)}) conditional(s32[]{:T(128)} %convert_element_type.2, (pred[]{:T(512)}, f32[448,128]{1,0:T(8,128)S(1)}) %tuple.25, () %tuple.26), branch_computations={%region_2.3_spmd, %region_3.4_spmd} | conditional | flops 57344 | bytes 1376265 | solution.py:265
  27.9 9.8 %all_gather.19 = f32[896,128]{1,0:T(8,128)S(1)} all-gather(f32[448,128]{1,0:T(8,128)S(1)} %get-tuple-element.29), channel_id=1, replica_groups={{0,2},{4,6},{8,10},{12,14},{16,18},{20,22},{24,26},{28,30},{32,34},{36,..., dimensions={0}, use_global_device_ids=true | all-gather | bytes 688128 | tf_op jit(solution)/shard_map/cond/branch_0_fun/all_gather | solution.py:251
  37.7 2.1 %all_gather.30.got_ref = f32[896,128]{1,0:T(8,128)S(1)} all-gather(f32[448,128]{1,0:T(8,128)S(1)} %get-tuple-element.49), channel_id=1, replica_groups={{0,1},{2,3},{4,5},{6,7},{8,9},{10,11},{12,13},{14,15},{16,17},{18,19},{..., dimensions={0}, use_global_device_ids=true | all-gather | bytes 688128 | tf_op jit(solution)/shard_map/all_gather | solution.py:251
  39.8 1.5 %next_step.3 = (f32[224,128]{1,0:T(8,128)S(1)}, f32[7,50,128]{2,1,0:T(8,128)S(1)}) custom-call(f32[448,128]{1,0:T(8,128)S(1)} %all_gather.29.own_ref, f32[896,128]{1,0:T(8,128)S(1)} %all_gather.30.got_ref, s32[30]{0:T(128)S(1)} %copy-done.3, s32[1,128]{1,0:T(1,128)S(1)} %bitcast.6, f32[7,50,128]{2,1,0:T(8,128)S(1)} %get-tuple-element.45.base_in, ...), custom_call_target="tpu_custom_call" | custom-call | tf_op jit(solution)/shard_map/next_step/pallas_call | solution.py:289
  41.3 2.0 %all_gather.31.own_ref = f32[448,128]{1,0:T(8,128)S(1)} all-gather(f32[224,128]{1,0:T(8,128)S(1)} %get-tuple-element.46), channel_id=1, replica_groups={{0,1},{2,3},{4,5},{6,7},{8,9},{10,11},{12,13},{14,15},{16,17},{18,19},{..., dimensions={0}, use_global_device_ids=true | all-gather | bytes 344064 | tf_op jit(solution)/shard_map/all_gather | solution.py:251
  43.3 9.8 %conditional.5 = (f32[448,128]{1,0:T(8,128)S(1)}) conditional(s32[]{:T(128)} %convert_element_type.2, (pred[]{:T(512)}, f32[448,128]{1,0:T(8,128)S(1)}) %tuple.27, () %tuple.28), branch_computations={%region_4.5_spmd, %region_5.6_spmd} | conditional | flops 57344 | bytes 1376265 | solution.py:265
  43.3 9.8 %all_gather.20 = f32[896,128]{1,0:T(8,128)S(1)} all-gather(f32[448,128]{1,0:T(8,128)S(1)} %get-tuple-element.31), channel_id=1, replica_groups={{0,2},{4,6},{8,10},{12,14},{16,18},{20,22},{24,26},{28,30},{32,34},{36,..., dimensions={0}, use_global_device_ids=true | all-gather | bytes 688128 | tf_op jit(solution)/shard_map/cond/branch_0_fun/all_gather | solution.py:251
  53.1 2.1 %all_gather.32.got_ref = f32[896,128]{1,0:T(8,128)S(1)} all-gather(f32[448,128]{1,0:T(8,128)S(1)} %get-tuple-element.50), channel_id=1, replica_groups={{0,1},{2,3},{4,5},{6,7},{8,9},{10,11},{12,13},{14,15},{16,17},{18,19},{..., dimensions={0}, use_global_device_ids=true | all-gather | bytes 688128 | tf_op jit(solution)/shard_map/all_gather | solution.py:251
  55.2 0.9 %last_step.1 = f32[7,50,128]{2,1,0:T(8,128)} custom-call(f32[448,128]{1,0:T(8,128)S(1)} %all_gather.31.own_ref, f32[896,128]{1,0:T(8,128)S(1)} %all_gather.32.got_ref, s32[1,128]{1,0:T(1,128)S(1)} %bitcast.7, f32[7,50,128]{2,1,0:T(8,128)S(1)} %get-tuple-element.47.base_in), custom_call_target="tpu_custom_call" | custom-call | tf_op jit(solution)/shard_map/last_step/pallas_call | solution.py:307
  (3 shorter events, 0.1 us)
Async XLA Ops:
  0.0 2.6 %copy-start = (bf16[30,128,128]{2,1,0:T(8,128)(2,1)S(1)}, bf16[30,128,128]{2,1,0:T(8,128)(2,1)}, u32[]{:S(2)}) copy-start(bf16[30,128,128]{2,1,0:T(8,128)(2,1)} %tiles_h.3) | copy-start | bytes 2949124
  0.0 2.6 %copy-start.3 = (s32[30]{0:T(128)S(1)}, s32[30]{0:T(128)}, u32[]{:S(2)}) copy-start(s32[30]{0:T(128)} %rows_h.5) | copy-start | bytes 364
  0.0 2.6 %copy-start.1 = (f32[3,7,50,128]{3,2,1,0:T(8,128)S(1)}, f32[3,7,50,128]{3,2,1,0:T(8,128)}, u32[]{:S(2)}) copy-start(f32[3,7,50,128]{3,2,1,0:T(8,128)} %states_h.5) | copy-start | bytes 1612804
  0.0 2.6 %copy-start.4 = (s32[30]{0:T(128)S(1)}, s32[30]{0:T(128)}, u32[]{:S(2)}) copy-start(s32[30]{0:T(128)} %param.19) | copy-start | bytes 364
  0.0 2.6 %copy-start.2 = (s32[128]{0:T(128)S(1)}, s32[128]{0:T(128)}, u32[]{:S(2)}) copy-start(s32[128]{0:T(128)} %param.17) | copy-start | bytes 1540

commit v6 on v5

--- a/solution.py
+++ b/solution.py
@@ -16,6 +16,7 @@
 time_step = 0.5
 SPAN = 32
 INFO = SLOTS
+KEPT = 10
 CHUNK = TRC * SPAN
 KEY = 64
 NONE = -1000.0
@@ -91,7 +92,7 @@
         base_ref[t] = carried[t] + time_step * bio[t]
 
 
-def make_terms(planes, tiles_ref, rows, sums, out_ref):
+def make_terms(planes, tile, rows, sums, out_ref):
     origin = lax.axis_index("col") * LEV
     for t in range(TRC):
         sums[t * SPAN + 24 : (t + 1) * SPAN, :] = jnp.zeros((8, 128), jnp.float32)
@@ -105,7 +106,7 @@
 
     for p in range(0, SLOTS, 2):
         left = jnp.concatenate(pick(p) + pick(p + 1), axis=0)
-        right = jnp.concatenate([tiles_ref[p], tiles_ref[p + 1]], axis=1)
+        right = jnp.concatenate([tile(p), tile(p + 1)], axis=1)
         prod = jnp.dot(left, right, preferred_element_type=jnp.float32)
         sums[pl.ds(p, 8, stride=SPAN), :] = prod[:8, :128] + prod[8:16, :128]
         sums[pl.ds(p + 1, 8, stride=SPAN), :] = prod[16:24, 128:] + prod[24:, 128:]
@@ -133,11 +134,12 @@
 
 
 def first_terms(rows_h, cols, count, wet, product_ref, states_h, implicit_h, tiles_ref,
-                out_ref, base_ref, upper, lower, planes, rows, states, sums, sems):
+                out_ref, base_ref, upper, lower, kept, planes, rows, states, sums, sems):
     halves = []
     for i, half in enumerate((upper, lower)):
         part = implicit_h.at[pl.ds(i * (LEV // 2), LEV // 2)]
         halves.append(pltpu.make_async_copy(part, half, sems.at[2 + i]))
+    halves.append(pltpu.make_async_copy(tiles_ref.at[pl.ds(0, KEPT)], kept, sems.at[4]))
     copy = pltpu.make_async_copy(rows_h, rows, sems.at[0])
     copy.start()
     for half in halves:
@@ -150,7 +152,7 @@
     lane = lax.broadcasted_iota(jnp.int32, (1, SLOTS), 1)
     code = jnp.where(lane < count[...], place + (KEY - LEV) * key, -1).astype(jnp.float32)
     copy.wait()
-    make_terms(planes, tiles_ref, rows, sums, out_ref)
+    make_terms(planes, lambda p: tiles_ref[p], rows, sums, out_ref)
     out_ref[INFO : INFO + 1, :] = jnp.full((1, 128), -1.0, jnp.float32)
     for i in range(128 // SPAN):
         out_ref[INFO : INFO + 1, i * SPAN : i * SPAN + SLOTS] = code
@@ -202,9 +204,9 @@
     receive(chunks_of(gots), take)
 
 
-def next_kernel(section, own_ref, got_ref, rows_h, wet_ref, base_in, upper, lower, states_h, tiles_h,
+def next_kernel(section, own_ref, got_ref, rows_h, wet_ref, base_in, upper, lower, kept, states_h, tiles_h,
                 out_ref, base_ref, planes, adj, rows, states, tiles_ref, sums, sems):
-    tile_copy = pltpu.make_async_copy(tiles_h, tiles_ref, sems.at[0])
+    tile_copy = pltpu.make_async_copy(tiles_h.at[pl.ds(KEPT, SLOTS - KEPT)], tiles_ref, sems.at[0])
     tile_copy.start()
     copy = pltpu.make_async_copy(rows_h, rows, sems.at[1])
     copy.start()
@@ -214,7 +216,7 @@
     carry(product(adj, upper, lower=lower), wet_ref[...], states, base_ref, planes, state_copy.wait)
     copy.wait()
     tile_copy.wait()
-    make_terms(planes, tiles_ref, rows, sums, out_ref)
+    make_terms(planes, lambda p: kept[p] if p < KEPT else tiles_ref[p - KEPT], rows, sums, out_ref)
     core = lax.rem(lax.axis_index("col"), 2)
     out_ref[INFO : INFO + 1, :] = own_ref[pl.ds(core * CHUNK + INFO, 1), :]
 
@@ -275,12 +277,12 @@
         name="first_step",
     )(final_adjoint, implicit)
     half = jax.ShapeDtypeStruct((LEV // 2, LEV, 128), f32)
-    terms, base, upper, lower = pl.pallas_call(
+    terms, base, upper, lower, kept = pl.pallas_call(
         first_terms,
         in_specs=[HBM] + [VMEM] * 4 + [HBM, HBM, VMEM],
-        out_specs=[VMEM] * 4,
-        out_shape=[slots, field, half, half],
-        scratch_shapes=[planes, rows, scratch, sums, pltpu.SemaphoreType.DMA((4,))],
+        out_specs=[VMEM] * 5,
+        out_shape=[slots, field, half, half, jax.ShapeDtypeStruct((KEPT, 128, 128), tiles.dtype)],
+        scratch_shapes=[planes, rows, scratch, sums, pltpu.SemaphoreType.DMA((5,))],
         compiler_params=pltpu.CompilerParams(vmem_limit_bytes=TERMS_GRANT),
         name="first_terms",
     )(tile_rows, tile_cols.reshape(1, SLOTS), tile_count.reshape(1, 1), wet, first, states, implicit, tiles)
@@ -288,7 +290,7 @@
         own, got = exchange(terms)
         terms, base = pl.pallas_call(
             functools.partial(next_kernel, section),
-            in_specs=[VMEM] * 2 + [HBM] + [VMEM] * 4 + [HBM, HBM],
+            in_specs=[VMEM] * 2 + [HBM] + [VMEM] * 5 + [HBM, HBM],
             out_specs=[VMEM] * 2,
             out_shape=[slots, field],
             scratch_shapes=[
@@ -296,13 +298,13 @@
                 scratch,
                 rows,
                 scratch,
-                pltpu.VMEM(tiles.shape, tiles.dtype),
+                pltpu.VMEM((SLOTS - KEPT, 128, 128), tiles.dtype),
                 sums,
                 pltpu.SemaphoreType.DMA((3,)),
             ],
             compiler_params=pltpu.CompilerParams(vmem_limit_bytes=NEXT_GRANT),
             name="next_step",
-        )(own, got, tile_rows, wet, base, upper, lower, states, tiles)
+        )(own, got, tile_rows, wet, base, upper, lower, kept, states, tiles)
     own, got = exchange(terms)
     return pl.pallas_call(
         last_kernel,

time: 56.5 us -> 56.3 us (level)
  no operation moved by 1% of the time
where the time goes in v6:
time: 56.3 us; the launch traced here: 56 us
  blocking collectives  48.1 us (85%)
  Pallas kernels  6.81 us (12%)
  between operations  0.9 us (2%)
    all_gather x9, blocking collectives, gather(): return lax.all_gather(x, 'col', axis_index_groups=groups, tiled=True)  48.1 us
    pallas_call x2, Pallas kernels, shards(): pl.pallas_call(functools.partial(next_kernel, section), in_specs=[VMEM] *...  2.78 us
    pallas_call x1, Pallas kernels, shards(): pl.pallas_call(first_kernel, in_specs=[HBM] * 2, out_specs=VMEM, out_shap...  1.78 us
    pallas_call x1, Pallas kernels, shards(): pl.pallas_call(first_terms, in_specs=[HBM] + [VMEM] * 4 + [HBM, HBM, VMEM...  1.33 us

profile of v6, /device:TPU:7, one launch (start us, length us, event | category | flops | bytes accessed | tf_op | source)
XLA Modules:
  0.0 56.0 jit_solution(11505463698904954971)
XLA Ops:
  0.0 0.0 copy-start
  0.0 0.0 copy-start.3
  0.0 0.0 copy-start.1
  0.0 0.0 copy-start.2
  0.0 0.0 copy-start.4
  0.8 1.8 %first_step.1.product_ref = f32[7,50,128]{2,1,0:T(8,128)S(1)} custom-call(f32[7,50,128]{2,1,0:T(8,128)} %final_h.1, f32[50,50,128]{2,1,0:T(8,128)} %implicit_h.3), custom_call_target="tpu_custom_call" | custom-call | tf_op jit(solution)/shard_map/first_step/pallas_call | solution.py:270
  2.6 0.0 copy-done
  2.6 0.0 copy-done.3
  2.6 0.0 copy-done.1
  2.6 0.0 copy-done.2
  2.6 0.0 copy-done.4
  2.6 1.3 %first_terms.1 = (f32[224,128]{1,0:T(8,128)S(1)}, f32[7,50,128]{2,1,0:T(8,128)S(1)}, f32[25,50,128]{2,1,0:T(8,128)S(1)}, f32[25,50,128]{2,1,0:T(8,128)S(1)}, bf16[10,128,128]{2,1,0:T(8,128)(2,1)S(1)}) custom-call(s32[30]{0:T(128)S(1)} %copy-done.3, s32[1,30]{1,0:T(1,128)S(1)} %bitcast.8, s32[1,1]{1,0:T(1,128)} %bitcast.3.count, s32[1,128]{1,0:T(1,128)S(1)} %bitcast.4, ...), custom_call_target="tpu_custom_call" | custom-call | tf_op jit(solution)/shard_map/first_terms/pallas_call | solution.py:280
  4.0 2.3 %all_gather.27.own_ref = f32[448,128]{1,0:T(8,128)S(1)} all-gather(f32[224,128]{1,0:T(8,128)S(1)} %get-tuple-element.41), channel_id=1, replica_groups={{0,1},{2,3},{4,5},{6,7},{8,9},{10,11},{12,13},{14,15},{16,17},{18,19},{..., dimensions={0}, use_global_device_ids=true | all-gather | bytes 344064 | tf_op jit(solution)/shard_map/all_gather | solution.py:253
  6.3 16.0 %conditional.3 = (f32[448,128]{1,0:T(8,128)S(1)}) conditional(s32[]{:T(128)} %convert_element_type.2, (pred[]{:T(512)}, f32[448,128]{1,0:T(8,128)S(1)}) %tuple.23, () %tuple.24), branch_computations={%region_0.1_spmd, %region_1.2_spmd} | conditional | flops 57344 | bytes 1376265 | solution.py:267
  6.3 16.0 %all_gather.18 = f32[896,128]{1,0:T(8,128)S(1)} all-gather(f32[448,128]{1,0:T(8,128)S(1)} %get-tuple-element.26), channel_id=1, replica_groups={{0,2},{4,6},{8,10},{12,14},{16,18},{20,22},{24,26},{28,30},{32,34},{36,..., dimensions={0}, use_global_device_ids=true | all-gather | bytes 688128 | tf_op jit(solution)/shard_map/cond/branch_0_fun/all_gather | solution.py:253
  22.3 2.1 %all_gather.28.got_ref = f32[896,128]{1,0:T(8,128)S(1)} all-gather(f32[448,128]{1,0:T(8,128)S(1)} %get-tuple-element.50), channel_id=1, replica_groups={{0,1},{2,3},{4,5},{6,7},{8,9},{10,11},{12,13},{14,15},{16,17},{18,19},{..., dimensions={0}, use_global_device_ids=true | all-gather | bytes 688128 | tf_op jit(solution)/shard_map/all_gather | solution.py:253
  24.4 1.4 %next_step.2 = (f32[224,128]{1,0:T(8,128)S(1)}, f32[7,50,128]{2,1,0:T(8,128)S(1)}) custom-call(f32[448,128]{1,0:T(8,128)S(1)} %all_gather.27.own_ref, f32[896,128]{1,0:T(8,128)S(1)} %all_gather.28.got_ref, s32[30]{0:T(128)S(1)} %copy-done.3, s32[1,128]{1,0:T(1,128)S(1)} %bitcast.5, f32[7,50,128]{2,1,0:T(8,128)S(1)} %get-tuple-element.42.base_in, ...), custom_call_target="tpu_custom_call" | custom-call | tf_op jit(solution)/shard_map/next_step/pallas_call | solution.py:291
  25.8 2.0 %all_gather.29.own_ref = f32[448,128]{1,0:T(8,128)S(1)} all-gather(f32[224,128]{1,0:T(8,128)S(1)} %get-tuple-element.46), channel_id=1, replica_groups={{0,1},{2,3},{4,5},{6,7},{8,9},{10,11},{12,13},{14,15},{16,17},{18,19},{..., dimensions={0}, use_global_device_ids=true | all-gather | bytes 344064 | tf_op jit(solution)/shard_map/all_gather | solution.py:253
  27.8 9.8 %conditional.4 = (f32[448,128]{1,0:T(8,128)S(1)}) conditional(s32[]{:T(128)} %convert_element_type.2, (pred[]{:T(512)}, f32[448,128]{1,0:T(8,128)S(1)}) %tuple.25, () %tuple.26), branch_computations={%region_2.3_spmd, %region_3.4_spmd} | conditional | flops 57344 | bytes 1376265 | solution.py:267
  27.8 9.8 %all_gather.19 = f32[896,128]{1,0:T(8,128)S(1)} all-gather(f32[448,128]{1,0:T(8,128)S(1)} %get-tuple-element.29), channel_id=1, replica_groups={{0,2},{4,6},{8,10},{12,14},{16,18},{20,22},{24,26},{28,30},{32,34},{36,..., dimensions={0}, use_global_device_ids=true | all-gather | bytes 688128 | tf_op jit(solution)/shard_map/cond/branch_0_fun/all_gather | solution.py:253
  37.6 2.1 %all_gather.30.got_ref = f32[896,128]{1,0:T(8,128)S(1)} all-gather(f32[448,128]{1,0:T(8,128)S(1)} %get-tuple-element.51), channel_id=1, replica_groups={{0,1},{2,3},{4,5},{6,7},{8,9},{10,11},{12,13},{14,15},{16,17},{18,19},{..., dimensions={0}, use_global_device_ids=true | all-gather | bytes 688128 | tf_op jit(solution)/shard_map/all_gather | solution.py:253
  39.7 1.4 %next_step.3 = (f32[224,128]{1,0:T(8,128)S(1)}, f32[7,50,128]{2,1,0:T(8,128)S(1)}) custom-call(f32[448,128]{1,0:T(8,128)S(1)} %all_gather.29.own_ref, f32[896,128]{1,0:T(8,128)S(1)} %all_gather.30.got_ref, s32[30]{0:T(128)S(1)} %copy-done.3, s32[1,128]{1,0:T(1,128)S(1)} %bitcast.6, f32[7,50,128]{2,1,0:T(8,128)S(1)} %get-tuple-element.47.base_in, ...), custom_call_target="tpu_custom_call" | custom-call | tf_op jit(solution)/shard_map/next_step/pallas_call | solution.py:291
  41.1 2.0 %all_gather.31.own_ref = f32[448,128]{1,0:T(8,128)S(1)} all-gather(f32[224,128]{1,0:T(8,128)S(1)} %get-tuple-element.48), channel_id=1, replica_groups={{0,1},{2,3},{4,5},{6,7},{8,9},{10,11},{12,13},{14,15},{16,17},{18,19},{..., dimensions={0}, use_global_device_ids=true | all-gather | bytes 344064 | tf_op jit(solution)/shard_map/all_gather | solution.py:253
  43.1 9.8 %conditional.5 = (f32[448,128]{1,0:T(8,128)S(1)}) conditional(s32[]{:T(128)} %convert_element_type.2, (pred[]{:T(512)}, f32[448,128]{1,0:T(8,128)S(1)}) %tuple.27, () %tuple.28), branch_computations={%region_4.5_spmd, %region_5.6_spmd} | conditional | flops 57344 | bytes 1376265 | solution.py:267
  43.1 9.8 %all_gather.20 = f32[896,128]{1,0:T(8,128)S(1)} all-gather(f32[448,128]{1,0:T(8,128)S(1)} %get-tuple-element.31), channel_id=1, replica_groups={{0,2},{4,6},{8,10},{12,14},{16,18},{20,22},{24,26},{28,30},{32,34},{36,..., dimensions={0}, use_global_device_ids=true | all-gather | bytes 688128 | tf_op jit(solution)/shard_map/cond/branch_0_fun/all_gather | solution.py:253
  52.9 2.1 %all_gather.32.got_ref = f32[896,128]{1,0:T(8,128)S(1)} all-gather(f32[448,128]{1,0:T(8,128)S(1)} %get-tuple-element.52), channel_id=1, replica_groups={{0,1},{2,3},{4,5},{6,7},{8,9},{10,11},{12,13},{14,15},{16,17},{18,19},{..., dimensions={0}, use_global_device_ids=true | all-gather | bytes 688128 | tf_op jit(solution)/shard_map/all_gather | solution.py:253
  55.0 0.9 %last_step.1 = f32[7,50,128]{2,1,0:T(8,128)} custom-call(f32[448,128]{1,0:T(8,128)S(1)} %all_gather.31.own_ref, f32[896,128]{1,0:T(8,128)S(1)} %all_gather.32.got_ref, s32[1,128]{1,0:T(1,128)S(1)} %bitcast.7, f32[7,50,128]{2,1,0:T(8,128)S(1)} %get-tuple-element.49.base_in), custom_call_target="tpu_custom_call" | custom-call | tf_op jit(solution)/shard_map/last_step/pallas_call | solution.py:309
  (3 shorter events, 0.1 us)
Async XLA Ops:
  0.0 2.6 %copy-start = (bf16[30,128,128]{2,1,0:T(8,128)(2,1)S(1)}, bf16[30,128,128]{2,1,0:T(8,128)(2,1)}, u32[]{:S(2)}) copy-start(bf16[30,128,128]{2,1,0:T(8,128)(2,1)} %tiles_h.3) | copy-start | bytes 2949124
  0.0 2.6 %copy-start.3 = (s32[30]{0:T(128)S(1)}, s32[30]{0:T(128)}, u32[]{:S(2)}) copy-start(s32[30]{0:T(128)} %rows_h.5) | copy-start | bytes 364
  0.0 2.6 %copy-start.1 = (f32[3,7,50,128]{3,2,1,0:T(8,128)S(1)}, f32[3,7,50,128]{3,2,1,0:T(8,128)}, u32[]{:S(2)}) copy-start(f32[3,7,50,128]{3,2,1,0:T(8,128)} %states_h.5) | copy-start | bytes 1612804
  0.0 2.6 %copy-start.2 = (s32[128]{0:T(128)S(1)}, s32[128]{0:T(128)}, u32[]{:S(2)}) copy-start(s32[128]{0:T(128)} %param.17) | copy-start | bytes 1540
  0.0 2.6 %copy-start.4 = (s32[30]{0:T(128)S(1)}, s32[30]{0:T(128)}, u32[]{:S(2)}) copy-start(s32[30]{0:T(128)} %param.19) | copy-start | bytes 364
